TPU v7x, 32 devices: a whole 2x2x4 slice. The times are simulated.
32 devices in a mesh: groups: 2 (over x), lat: 16 (over z, y, core).
Axes of the slice: x: 2, y: 2, z: 4, core: 2. Of those that a mesh axis runs over, the one named last changes fastest.
Arguments:
- state_field: bfloat16 [96, 1440, 256], P(('groups', 'lat')), parts along dimension 0, may hold values from -6 to 6
- filter_values: float32 [48, 3, 2, 8, 3], P('lat'), may hold values from -0.8 to 0.8
- block_index: int32 [48, 3, 2], P('lat'), may hold values from 0 to 179
- disco_mix: bfloat16 [768, 256], replicated, may hold values from -0.21875 to 0.21875
- spectral_gain: float32 [48, 256], replicated, may hold values from 0.1 to 1.9
- spectral_weight: bfloat16 [2, 256, 256], replicated, may hold values from -0.25 to 0.25
Outputs:
- block_out: bfloat16 [96, 1440, 256], P(('groups', 'lat')), parts along dimension 0
There are 2 independent parts, one for each index of `groups`. A program takes and returns all parts, laid end to end along the dimension named above; an argument that names none is the same for every part. Nothing has to cross between parts.
Inputs may be any that keep to these rules, and one draw needn't show every extreme that they name: `block_index`: block b stands for the longitude shifts 8 * b to 8 * b + 7; two entries of one cycle and offset may name the same block.
All inputs are finite; a program needn't handle non-finite values.
Results may differ from a plain program's by a relative error of at most 0.008.
Values may be sent and summed in bfloat16 or wider, within the bound.
A program may use at most 256 MiB of HBM per device.

v0:
```python
import math

import jax
import jax.numpy as jnp
from jax import lax
from jax.sharding import PartitionSpec as P

M_DEV = 3
KB = 3
SB = 8


log_cut = -69.0


def with_halo(shard, sides, width):
    for axis, dim in sides:
        count, length = (lax.axis_size(axis), shard.shape[dim])
        up = [(i, (i + 1) % count) for i in range(count - 1)]
        down = [(j, i) for i, j in up]
        last = lax.slice_in_dim(shard, length - width, length, axis=dim)
        leading = lax.slice_in_dim(shard, 0, width, axis=dim)
        before = lax.ppermute(last, axis, up)
        after = lax.ppermute(leading, axis, down)
        shard = jnp.concatenate([before, shard, after], axis=dim)
    return shard


def legendre_table(wave_orders, degree_count, lat_count):
    colatitude = (jnp.arange(lat_count, dtype=jnp.float32) + 0.5) * (math.pi / lat_count)
    cosine = jnp.cos(colatitude)[None, :]
    sine_col = jnp.sin(colatitude)[None, :]
    orders = wave_orders.astype(jnp.float32)[:, None]
    log_first = (
        0.5 * (jnp.log(2.0 * orders + 1.0) - math.log(4.0 * math.pi))
        + 0.5 * (lax.lgamma(orders + 0.5) - 0.5 * math.log(math.pi) - lax.lgamma(orders + 1.0))
        + orders * jnp.log(sine_col)
    )
    first_term = jnp.where(log_first < log_cut, 0.0, jnp.exp(log_first))

    def advance(state_pair, degree):
        before, current = state_pair
        deg_sq = degree * degree
        ord_sq = orders * orders
        lower_deg = degree - 1.0
        coef_up = jnp.sqrt((4.0 * deg_sq - 1.0) / jnp.maximum(deg_sq - ord_sq, 1.0))
        coef_down = jnp.sqrt(
            jnp.maximum(lower_deg * lower_deg - ord_sq, 0.0)
            / jnp.maximum(4.0 * lower_deg * lower_deg - 1.0, 1.0)
        )
        general = coef_up * (cosine * current - coef_down * before)
        second = jnp.sqrt(2.0 * orders + 3.0) * cosine * current
        next_value = jnp.where(
            degree < orders,
            0.0,
            jnp.where(
                degree == orders, first_term, jnp.where(degree == orders + 1.0, second, general)
            ),
        )
        return ((current, next_value), next_value)

    zeros_state = jnp.zeros((orders.shape[0], lat_count), jnp.float32)
    degrees = jnp.arange(degree_count, dtype=jnp.float32)
    final_state, table_rows = lax.scan(advance, (zeros_state, zeros_state), degrees, unroll=16)
    return jnp.transpose(table_rows, (1, 0, 2))


def quad_weights(lat_count):
    colatitude = (jnp.arange(lat_count, dtype=jnp.float32) + 0.5) * (math.pi / lat_count)
    return jnp.sin(colatitude) * (2.0 * math.pi * math.pi / lat_count)


def forward_table(waves, lon_count):
    longitude = jnp.arange(lon_count, dtype=jnp.int32)
    angles = (longitude[:, None] * waves[None, :] % lon_count).astype(jnp.float32) * (
        2.0 * math.pi / lon_count
    )
    paired = jnp.stack([jnp.cos(angles), -jnp.sin(angles)], axis=2) / lon_count
    return paired.reshape(lon_count, 2 * waves.shape[0]).astype(jnp.bfloat16)


def inverse_table(waves, lon_count):
    longitude = jnp.arange(lon_count, dtype=jnp.int32)
    angles = (waves[:, None] * longitude[None, :] % lon_count).astype(jnp.float32) * (
        2.0 * math.pi / lon_count
    )
    factor = jnp.where(waves == 0, 1.0, 2.0).astype(jnp.float32)[:, None]
    paired = jnp.stack([factor * jnp.cos(angles), -factor * jnp.sin(angles)], axis=1)
    return paired.reshape(2 * waves.shape[0], lon_count).astype(jnp.bfloat16)


def shift_matrix(filters, shift_block):
    shift_ids = jnp.arange(shift_block, dtype=jnp.int32)
    cell_ids = jnp.arange(2 * shift_block, dtype=jnp.int32)
    pick = (
        shift_ids[:, None, None] == shift_ids[None, :, None] + shift_block - cell_ids[None, None, :]
    ).astype(jnp.float32)
    basis_count = filters.shape[-1]
    table = jnp.einsum("gjtk,tuw->gjwuk", filters, pick, precision=lax.Precision.HIGHEST)
    return table.reshape(
        filters.shape[0] * filters.shape[1] * 2 * shift_block, shift_block * basis_count
    )


def cycle_windows(cycles, blocks, shift_block):
    lon_count = cycles.shape[1]

    def one_window(cycle_data, block_number):
        doubled = jnp.concatenate([cycle_data, cycle_data], axis=0)
        start_cell = lon_count - shift_block * (block_number + 1)
        piece = lax.dynamic_slice_in_dim(doubled, start_cell, lon_count + shift_block, 0)
        piece = piece.reshape(lon_count // shift_block + 1, shift_block, cycle_data.shape[1])
        return jnp.concatenate([piece[:-1], piece[1:]], axis=1)

    def per_offset(cycle_data, block_row):
        return jax.vmap(one_window, in_axes=(None, 0))(cycle_data, block_row)

    windows = jax.vmap(per_offset)(cycles, blocks)
    group_count, slot_count, block_count, width, channels = windows.shape
    return jnp.transpose(windows, (2, 0, 1, 3, 4)).reshape(
        block_count, group_count * slot_count * width, channels
    )


def disco_part(sources, filters, blocks, shift_block):
    lon_count = sources.shape[2]
    channels = sources.shape[3]
    basis_count = filters.shape[-1]

    def one_cycle(operands):
        cycle_group, cycle_filters, cycle_blocks = operands
        windows = cycle_windows(cycle_group.astype(jnp.float32), cycle_blocks, shift_block)
        table = shift_matrix(cycle_filters, shift_block)
        result = jnp.einsum("avc,vw->awc", windows, table, precision=lax.Precision.HIGHEST)
        return result.reshape(lon_count, basis_count, channels)

    return lax.map(one_cycle, (sources, filters, blocks))


def body(state_field, filter_values, block_index, disco_mix, spectral_gain, spectral_weight):
    cycle_count = state_field.shape[0]
    lon_count = state_field.shape[1]
    channels = state_field.shape[2]
    lat_devices = lax.axis_size("lat")
    lat_count = cycle_count * lat_devices
    mode_count = M_DEV * lat_devices
    tile_rows = min(128, lat_count)
    padded = with_halo(state_field, (("lat", 0),), 1)
    sources = jnp.stack(
        [padded[0:cycle_count], padded[1 : cycle_count + 1], padded[2 : cycle_count + 2]], axis=1
    )
    summed = disco_part(sources, filter_values, block_index, SB)
    basis_terms = summed.reshape(cycle_count, lon_count, KB * channels).astype(jnp.bfloat16)
    local_mix = jnp.einsum(
        "rlk,kc->rlc", basis_terms, disco_mix, preferred_element_type=jnp.float32
    ).astype(jnp.bfloat16)
    all_slots = jnp.arange(mode_count, dtype=jnp.int32)
    own_slots = lax.axis_index("lat") * M_DEV + jnp.arange(M_DEV, dtype=jnp.int32)
    table_fwd = forward_table(all_slots, lon_count)
    spectrum = jnp.einsum(
        "lq,rlc->rqc", table_fwd, local_mix, preferred_element_type=jnp.float32
    ).astype(jnp.bfloat16)
    owners = lax.all_to_all(spectrum, "lat", split_axis=1, concat_axis=0, tiled=True)
    slot_inputs = jnp.transpose(owners.reshape(lat_count, M_DEV, 2 * channels), (1, 0, 2))
    slot_tables = legendre_table(own_slots, lat_count, lat_count)
    quadrature = quad_weights(lat_count)
    real_part = spectral_weight[0]
    imag_part = spectral_weight[1]
    big_weight = jnp.concatenate(
        [
            jnp.concatenate([real_part, imag_part], axis=1),
            jnp.concatenate([-imag_part, real_part], axis=1),
        ],
        axis=0,
    )

    def process_slot(operands):
        slot_table, slot_data, slot_wave = operands
        data_wide = slot_data.astype(jnp.float32)

        def tile_step(tile_index, running):
            first_row = tile_index * tile_rows
            legendre_rows = lax.dynamic_slice_in_dim(slot_table, first_row, tile_rows, 0)
            coefficients = jnp.dot(
                legendre_rows * quadrature[None, :], data_wide, precision=lax.Precision.HIGHEST
            )
            gain_rows = lax.dynamic_slice_in_dim(spectral_gain, first_row, tile_rows, 0)
            scaled = (
                (coefficients.reshape(tile_rows, 2, channels) * gain_rows[:, None, :])
                .reshape(tile_rows, 2 * channels)
                .astype(jnp.bfloat16)
            )
            mixed_rows = jnp.dot(scaled, big_weight, preferred_element_type=jnp.float32)
            return running + jnp.dot(legendre_rows.T, mixed_rows, precision=lax.Precision.HIGHEST)

        start_tile = slot_wave // tile_rows
        result = lax.fori_loop(
            start_tile,
            lat_count // tile_rows,
            tile_step,
            jnp.zeros((lat_count, 2 * channels), jnp.float32),
        )
        return result.astype(jnp.bfloat16)

    synthesis = lax.map(process_slot, (slot_tables, slot_inputs, own_slots))
    synthesis = jnp.transpose(synthesis, (1, 0, 2)).reshape(lat_count, 2 * M_DEV, channels)
    returned = lax.all_to_all(synthesis, "lat", split_axis=0, concat_axis=1, tiled=True)
    table_inv = inverse_table(all_slots, lon_count)
    global_part = jnp.einsum("rqc,ql->rlc", returned, table_inv, preferred_element_type=jnp.float32)
    return jax.nn.gelu(local_mix.astype(jnp.float32) + global_part).astype(jnp.bfloat16)


def solution(mesh):
    return jax.shard_map(
        body,
        mesh=mesh,
        in_specs=(
            P(("groups", "lat"), None, None),
            P("lat", None, None, None, None),
            P("lat", None, None),
            P(),
            P(),
            P(),
        ),
        out_specs=P(("groups", "lat"), None, None),
        check_vma=False,
    )
```

profile of v0, /device:TPU:13, one launch (start us, length us, event | category | flops | bytes accessed | tf_op | source)
XLA Modules:
  0.0 462.3 jit_solution(11374386352443968915)
XLA Ops:
  9.1 158.7 %while.72 = (s32[]{:T(128)}, f32[3,48]{1,0:T(4,128)S(1)}, f32[3,48]{1,0:T(4,128)S(1)}, f32[3,16,3,48]{3,2,1,0:T(4,128)}, f32[3,16]{1,0:T(4,128)S(1)}, /*index=5*...) while((s32[]{:T(128)}, f32[3,48]{1,0:T(4,128)S(1)}, ...), condition=%wide.region_3.4_spmd.clone.clone.clone.clone, body=%wide.region_2.3_spmd.clone.clone.clone.clone.sunk | while | flops 31409 | bytes 251289 | solution.py:64
  176.7 216.0 %while.69 = (s32[]{:T(128)}, bf16[3,1440,3,256]{3,2,1,0:T(4,128)(2,1)}, f32[3,3,2,8,3]{3,2,4,1,0:T(2,128)}, bf16[3,3,1440,256]{3,2,1,0:T(8,128)(2,1)}, s32[3,3,2...) while((s32[]{:T(128)}, bf16[3,1440,3,256]{3,2,1,0:T(4,128)(2,1)}, f32[3,3,2,8,3]{3,2,4,1,0:T(2,128)}, ...), condition=%wide.region_1.2_spmd, body=%wide.region_0.1_spmd.sunk | while | flops 1287513344 | bytes 154168800 | solution.py:137
  183.5 27.3 %while.73 = (s32[]{:T(128)}, f32[3,2880,256]{2,1,0:T(8,128)}, s32[6,3]{0,1:T(4,128)S(1)}, f32[6,1448,256]{2,1,0:T(8,128)}, s32[]{:T(128)}) while((s32[]{:T(128)}, f32[3,2880,256]{2,1,0:T(8,128)}, s32[6,3]{0,1:T(4,128)S(1)}, f32[6,1448,256]{2,1,0:T(8,128)}, s32[]{:T(128)}) %tuple.342), condition=%wide.while_cond, body=%wide.while_body.sunk | while | flops 2 | bytes 2967145 | solution.py:111
  210.9 7.3 %fusion.162 = (f32[3,2,180,8,256]{4,3,2,1,0:T(8,128)S(1)}, f32[3,2,180,8,256]{4,3,2,1,0:T(8,128)S(1)}) fusion(f32[3,2,181,8,256]{4,3,2,1,0:T(8,128)} %bitcast.509), kind=kLoop, calls=%fused_computation.303.clone.1 | loop fusion | bytes 35389440 | tf_op jit(solution)/shard_map/while/body/eval_jaxpr/vmap(vmap())/slice | solution.py:113
  219.8 7.4 %copy.105 = f32[3,2,180,16,256]{4,3,1,0,2:T(8,128)} copy(f32[3,2,180,16,256]{4,3,2,1,0:T(8,128)S(1)} %pad_maximum_fusion.6) | data formatting | bytes 35389440 | tf_op jit(solution)/shard_map/while/body/eval_jaxpr/vmap(vmap())/concatenate | solution.py:113
  228.4 12.2 %convolution_bitcast_fusion.5 = bf16[180,24,256]{2,1,0:T(8,128)(2,1)} fusion(f32[96,24,1]{0,1,2:T(8,128)S(1)} %reshape.1697, f32[180,96,256]{2,1,0:T(8,128)} %bitcast.508), kind=kOutput, calls=%fused_computation.11.clone.1 | convolution fusion | flops 1274019840 | bytes 19915776 | tf_op jit(solution)/shard_map/while/body/eval_jaxpr/avc,vw->awc/dot_general | solution.py:134
  240.6 5.3 %broadcast_in_dim.1124 = bf16[1,1440,3,256]{3,2,1,0:T(4,128)(2,1)S(1)} reshape(bf16[180,24,256]{2,1,0:T(8,128)(2,1)} %convolution_bitcast_fusion.5) | data formatting | bytes 4423680 | tf_op jit(solution)/shard_map/while/body/jit(dynamic_update_index_in_dim)/broadcast_in_dim | solution.py:137
  250.4 4.2 maximum_convert_fusion.2
  255.5 27.3 %while.73 = (s32[]{:T(128)}, f32[3,2880,256]{2,1,0:T(8,128)}, s32[6,3]{0,1:T(4,128)S(1)}, f32[6,1448,256]{2,1,0:T(8,128)}, s32[]{:T(128)}) while((s32[]{:T(128)}, f32[3,2880,256]{2,1,0:T(8,128)}, s32[6,3]{0,1:T(4,128)S(1)}, f32[6,1448,256]{2,1,0:T(8,128)}, s32[]{:T(128)}) %tuple.342), condition=%wide.while_cond, body=%wide.while_body.sunk | while | flops 2 | bytes 2967145 | solution.py:111
  282.8 7.3 %fusion.162 = (f32[3,2,180,8,256]{4,3,2,1,0:T(8,128)S(1)}, f32[3,2,180,8,256]{4,3,2,1,0:T(8,128)S(1)}) fusion(f32[3,2,181,8,256]{4,3,2,1,0:T(8,128)} %bitcast.509), kind=kLoop, calls=%fused_computation.303.clone.1 | loop fusion | bytes 35389440 | tf_op jit(solution)/shard_map/while/body/eval_jaxpr/vmap(vmap())/slice | solution.py:113
  291.8 7.4 %copy.105 = f32[3,2,180,16,256]{4,3,1,0,2:T(8,128)} copy(f32[3,2,180,16,256]{4,3,2,1,0:T(8,128)S(1)} %pad_maximum_fusion.6) | data formatting | bytes 35389440 | tf_op jit(solution)/shard_map/while/body/eval_jaxpr/vmap(vmap())/concatenate | solution.py:113
  300.4 12.2 %convolution_bitcast_fusion.5 = bf16[180,24,256]{2,1,0:T(8,128)(2,1)} fusion(f32[96,24,1]{0,1,2:T(8,128)S(1)} %reshape.1697, f32[180,96,256]{2,1,0:T(8,128)} %bitcast.508), kind=kOutput, calls=%fused_computation.11.clone.1 | convolution fusion | flops 1274019840 | bytes 19915776 | tf_op jit(solution)/shard_map/while/body/eval_jaxpr/avc,vw->awc/dot_general | solution.py:134
  312.6 5.3 %broadcast_in_dim.1124 = bf16[1,1440,3,256]{3,2,1,0:T(4,128)(2,1)S(1)} reshape(bf16[180,24,256]{2,1,0:T(8,128)(2,1)} %convolution_bitcast_fusion.5) | data formatting | bytes 4423680 | tf_op jit(solution)/shard_map/while/body/jit(dynamic_update_index_in_dim)/broadcast_in_dim | solution.py:137
  327.5 27.3 %while.73 = (s32[]{:T(128)}, f32[3,2880,256]{2,1,0:T(8,128)}, s32[6,3]{0,1:T(4,128)S(1)}, f32[6,1448,256]{2,1,0:T(8,128)}, s32[]{:T(128)}) while((s32[]{:T(128)}, f32[3,2880,256]{2,1,0:T(8,128)}, s32[6,3]{0,1:T(4,128)S(1)}, f32[6,1448,256]{2,1,0:T(8,128)}, s32[]{:T(128)}) %tuple.342), condition=%wide.while_cond, body=%wide.while_body.sunk | while | flops 2 | bytes 2967145 | solution.py:111
  354.8 7.3 %fusion.162 = (f32[3,2,180,8,256]{4,3,2,1,0:T(8,128)S(1)}, f32[3,2,180,8,256]{4,3,2,1,0:T(8,128)S(1)}) fusion(f32[3,2,181,8,256]{4,3,2,1,0:T(8,128)} %bitcast.509), kind=kLoop, calls=%fused_computation.303.clone.1 | loop fusion | bytes 35389440 | tf_op jit(solution)/shard_map/while/body/eval_jaxpr/vmap(vmap())/slice | solution.py:113
  363.8 7.4 %copy.105 = f32[3,2,180,16,256]{4,3,1,0,2:T(8,128)} copy(f32[3,2,180,16,256]{4,3,2,1,0:T(8,128)S(1)} %pad_maximum_fusion.6) | data formatting | bytes 35389440 | tf_op jit(solution)/shard_map/while/body/eval_jaxpr/vmap(vmap())/concatenate | solution.py:113
  372.3 12.2 %convolution_bitcast_fusion.5 = bf16[180,24,256]{2,1,0:T(8,128)(2,1)} fusion(f32[96,24,1]{0,1,2:T(8,128)S(1)} %reshape.1697, f32[180,96,256]{2,1,0:T(8,128)} %bitcast.508), kind=kOutput, calls=%fused_computation.11.clone.1 | convolution fusion | flops 1274019840 | bytes 19915776 | tf_op jit(solution)/shard_map/while/body/eval_jaxpr/avc,vw->awc/dot_general | solution.py:134
  384.6 5.3 %broadcast_in_dim.1124 = bf16[1,1440,3,256]{3,2,1,0:T(4,128)(2,1)S(1)} reshape(bf16[180,24,256]{2,1,0:T(8,128)(2,1)} %convolution_bitcast_fusion.5) | data formatting | bytes 4423680 | tf_op jit(solution)/shard_map/while/body/jit(dynamic_update_index_in_dim)/broadcast_in_dim | solution.py:137
  392.6 14.4 %copy.65 = bf16[3,1440,3,256]{1,3,2,0:T(8,128)(2,1)} copy(bf16[3,1440,3,256]{3,2,1,0:T(4,128)(2,1)} %get-tuple-element.503) | data formatting | bytes 13271040 | tf_op jit(solution)/shard_map/convert_element_type | solution.py:153
  407.0 5.1 %convolution_convert_fusion = bf16[3,1440,256]{2,1,0:T(8,128)(2,1)S(1)} fusion(bf16[3,1440,768]{1,2,0:T(8,128)(2,1)} %bitcast.513, bf16[768,256]{1,0:T(8,128)(2,1)S(1)} %copy-done), kind=kOutput, calls=%fused_computation.225 | convolution fusion | flops 1699799040 | bytes 9240576 | tf_op jit(solution)/shard_map/rlk,kc->rlc/dot_general | solution.py:154
  413.5 6.5 %all-to-all-start = ((bf16[3,96,256]{2,0,1:T(4,128)(2,1)}), bf16[3,96,256]{2,0,1:T(4,128)(2,1)S(1)}, u32[]{:S(2)}, u32[]{:S(2)}) async-start(bf16[3,96,256]{2,0,1:T(4,128)(2,1)} %copy.70), calls=%async_computation | async-start | bytes 393216 | tf_op jit(solution)/shard_map/all_to_all | solution.py:163
  422.0 4.5 all-to-all-done
  429.0 14.6 %while.71 = (s32[]{:T(128)}, bf16[3,48,512]{2,1,0:T(8,128)(2,1)}, s32[3]{0:T(128)S(1)}, f32[3,48,48]{2,1,0:T(8,128)S(1)}, bf16[3,48,512]{2,1,0:T(8,128)(2,1)}, /...) while((s32[]{:T(128)}, bf16[3,48,512]{2,1,0:T(8,128)(2,1)}, ...), condition=%wide.region_7.8_spmd.clone, body=%wide.region_4.7_spmd.clone.sunk | while | flops 53578136 | bytes 2001404 | solution.py:205
  445.4 5.9 %all-to-all-start.1 = ((bf16[48,6,256]{2,1,0:T(8,128)(2,1)}), bf16[48,6,256]{2,1,0:T(8,128)(2,1)S(1)}, u32[]{:S(2)}, u32[]{:S(2)}) async-start(bf16[48,6,256]{2,1,0:T(8,128)(2,1)} %reshape.1657), calls=%async_computation.1 | async-start | bytes 393216 | tf_op jit(solution)/shard_map/all_to_all | solution.py:207
  (371 shorter events, 228.8 us)
Async XLA Ops:
  0.0 407.0 %copy-start = (bf16[768,256]{1,0:T(8,128)(2,1)S(1)}, bf16[768,256]{1,0:T(8,128)(2,1)}, u32[]{:S(2)}) copy-start(bf16[768,256]{1,0:T(8,128)(2,1)} %param.17) | copy-start | bytes 1179652
  2.7 167.6 %copy-start.4 = (bf16[2,256,256]{2,1,0:T(8,128)(2,1)S(1)}, bf16[2,256,256]{2,1,0:T(8,128)(2,1)}, u32[]{:S(2)}) copy-start(bf16[2,256,256]{2,1,0:T(8,128)(2,1)} %param.19) | copy-start | bytes 786436
  2.7 169.0 %copy-start.1 = (bf16[3,1440,256]{2,1,0:T(8,128)(2,1)S(1)}, bf16[3,1440,256]{2,1,0:T(8,128)(2,1)}, u32[]{:S(2)}) copy-start(bf16[3,1440,256]{2,1,0:T(8,128)(2,1)} %param.14) | copy-start | bytes 6635524
  2.7 169.0 %collective-permute-start = (bf16[1,1440,256]{2,1,0:T(8,128)(2,1)}, bf16[1,1440,256]{2,1,0:T(8,128)(2,1)}, u32[]{:S(2)}, u32[]{:S(2)}) collective-permute-start(bf16[1,1440,256]{2,1,0:T(8,128)(2,1)} %get-tuple-element.926), channel_id=1, source_target_pairs={{0,1},{1,2},{2,3},{3,4},{4,5},{5,6},{6,7},{7,8},{8,9},{9,10},{10,1... | collective-permute-start | bytes 2211848 | tf_op jit(solution)/shard_map/ppermute | solution.py:23
  6.5 165.2 %collective-permute-start.1 = (bf16[1,1440,256]{2,1,0:T(8,128)(2,1)}, bf16[1,1440,256]{2,1,0:T(8,128)(2,1)}, u32[]{:S(2)}, u32[]{:S(2)}) collective-permute-start(bf16[1,1440,256]{2,1,0:T(8,128)(2,1)} %get-tuple-element.927), channel_id=1, source_target_pairs={{1,0},{2,1},{3,2},{4,3},{5,4},{6,5},{7,6},{8,7},{9,8},{10,9},{11,1... | collective-permute-start | bytes 2211848 | tf_op jit(solution)/shard_map/ppermute | solution.py:24
  407.0 5.1 %copy-start.3 = (bf16[1440,96,1]{0,1,2:T(8,128)(2,1)S(1)}, bf16[1440,96,1]{0,1,2:T(8,128)(2,1)}, u32[]{:S(2)}) copy-start(bf16[1440,96,1]{0,1,2:T(8,128)(2,1)} %reshape.1686) | copy-start | bytes 829444
  412.1 16.8 %copy-start.2 = (f32[48,256]{1,0:T(8,128)S(1)}, f32[48,256]{1,0:T(8,128)}, u32[]{:S(2)}) copy-start(f32[48,256]{1,0:T(8,128)} %param.18) | copy-start | bytes 147460
  412.1 16.8 %copy-start.5 = (s32[3]{0:T(128)S(1)}, s32[3]{0:T(128)}, u32[]{:S(2)}) copy-start(s32[3]{0:T(128)} %get-tuple-element.1487) | copy-start | bytes 40
  413.5 13.0 %all-to-all-start = ((bf16[3,96,256]{2,0,1:T(4,128)(2,1)}), bf16[3,96,256]{2,0,1:T(4,128)(2,1)S(1)}, u32[]{:S(2)}, u32[]{:S(2)}) async-start(bf16[3,96,256]{2,0,1:T(4,128)(2,1)} %copy.70), calls=%async_computation | async-start | bytes 393216 | tf_op jit(solution)/shard_map/all_to_all | solution.py:163
  445.4 12.5 %all-to-all-start.1 = ((bf16[48,6,256]{2,1,0:T(8,128)(2,1)}), bf16[48,6,256]{2,1,0:T(8,128)(2,1)S(1)}, u32[]{:S(2)}, u32[]{:S(2)}) async-start(bf16[48,6,256]{2,1,0:T(8,128)(2,1)} %reshape.1657), calls=%async_computation.1 | async-start | bytes 393216 | tf_op jit(solution)/shard_map/all_to_all | solution.py:207
where the time goes:
time: 470 us; the launch traced here: 462 us
  local copies, waits for them, and re-layouts  191 us (41%)
  other arithmetic  96.9 us (21%)
  loops' own time  96 us (20%)
  matrix products  51.6 us (11%)
  starting transfers between devices  18.1 us (4%)
  waiting for transfers between devices  8.5 us (2%)
    another operation x1, loops' own time, legendre_table(): lax.scan(advance, (zeros_state, zeros_state), degrees, unroll=16)  89.8 us
    gather x54, local copies, waits for them, and re-layouts  82 us
    dot_general x3, matrix products, one_cycle(): jnp.einsum('avc,vw->awc', windows, table, precision=lax.Precision.HIGHEST)  36.7 us
    lt x24, other arithmetic, advance(): degree < orders  29.7 us
    concatenate x3, local copies, waits for them, and re-layouts, one_window(): return jnp.concatenate([piece[:-1], piece[1:]], axis=1)  22.2 us
    slice x3, local copies, waits for them, and re-layouts, one_window(): return jnp.concatenate([piece[:-1], piece[1:]], axis=1)  21.9 us
    broadcast_in_dim x3, local copies, waits for them, and re-layouts, disco_part(): return lax.map(one_cycle, (sources, filters, blocks))  16 us
    eq x24, other arithmetic, advance(): degree == orders  15.6 us
  transfers between devices with their start and end apart: 4, of which 2 were waited for; matrix products, arithmetic and copies ran while one was open for 17% of the time, Pallas kernels for 0%

commit v1 on v0

v1 whole, which is shorter than its diff:
```python
import functools
import math

import jax
import jax.numpy as jnp
import ml_dtypes
import numpy as np
from jax import lax
from jax.experimental import pallas as pl
from jax.experimental.pallas import tpu as pltpu
from jax.sharding import PartitionSpec as P

M_DEV = 3
KB = 3
SB = 8
ROWS = 96
WIN = 128
CHUNK = 48
BLK = 32
log_cut = -69.0
MESH = pl.DeviceIdType.MESH
F32 = jnp.float32
BF16 = jnp.bfloat16


def legendre_np(count):
    theta = (np.arange(count) + 0.5) * (math.pi / count)
    cosine, sine = np.cos(theta)[None], np.sin(theta)[None]
    m = np.arange(count, dtype=np.float64)[:, None]
    lg = np.array([math.lgamma(x + 0.5) - math.lgamma(x + 1.0) for x in range(count)])[:, None]
    g = 0.5 * (np.log(2 * m + 1) - math.log(4 * math.pi)) + 0.5 * (lg - 0.5 * math.log(math.pi)) + m * np.log(sine)
    first = np.where(g < log_cut, 0.0, np.exp(g))
    table = np.zeros((count, count, count))
    before = current = np.zeros((count, count))
    for l in range(count):
        up = np.sqrt((4.0 * l * l - 1.0) / np.maximum(l * l - m * m, 1.0)) if l else 0.0 * m
        down = np.sqrt(np.maximum((l - 1.0) ** 2 - m * m, 0.0) / max(4.0 * (l - 1.0) ** 2 - 1.0, 1.0))
        general = up * (cosine * current - down * before)
        second = np.sqrt(2 * m + 3) * cosine * current
        value = np.where(l < m, 0.0, np.where(l == m, first, np.where(l == m + 1, second, general)))
        before, current = current, value
        table[:, l] = value
    return table


def legendre_table(wave_orders, degree_count, lat_count):
    colatitude = (jnp.arange(lat_count, dtype=F32) + 0.5) * (math.pi / lat_count)
    cosine = jnp.cos(colatitude)[None, :]
    sine_col = jnp.sin(colatitude)[None, :]
    orders = wave_orders.astype(F32)[:, None]
    log_first = (
        0.5 * (jnp.log(2.0 * orders + 1.0) - math.log(4.0 * math.pi))
        + 0.5 * (lax.lgamma(orders + 0.5) - 0.5 * math.log(math.pi) - lax.lgamma(orders + 1.0))
        + orders * jnp.log(sine_col)
    )
    first_term = jnp.where(log_first < log_cut, 0.0, jnp.exp(log_first))

    def advance(state_pair, degree):
        before, current = state_pair
        deg_sq = degree * degree
        ord_sq = orders * orders
        lower_deg = degree - 1.0
        coef_up = jnp.sqrt(jnp.maximum(4.0 * deg_sq - 1.0, 0.0) / jnp.maximum(deg_sq - ord_sq, 1.0))
        coef_down = jnp.sqrt(
            jnp.maximum(lower_deg * lower_deg - ord_sq, 0.0)
            / jnp.maximum(4.0 * lower_deg * lower_deg - 1.0, 1.0)
        )
        general = coef_up * (cosine * current - coef_down * before)
        second = jnp.sqrt(2.0 * orders + 3.0) * cosine * current
        next_value = jnp.where(
            degree < orders,
            0.0,
            jnp.where(
                degree == orders, first_term, jnp.where(degree == orders + 1.0, second, general)
            ),
        )
        return ((current, next_value), next_value)

    zeros_state = jnp.zeros((orders.shape[0], lat_count), F32)
    degrees = jnp.arange(degree_count, dtype=F32)
    _, table_rows = lax.scan(advance, (zeros_state, zeros_state), degrees)
    return jnp.transpose(table_rows, (1, 0, 2))


def spread(xp, table, quad, devices):
    count = table.shape[1]
    chunks = count // CHUNK
    lat = xp.arange(count)[:, None]
    col = xp.arange(devices * BLK)[None, :]
    here = (lat == 3 * (col // BLK) + col % BLK // 8) & (col % BLK < 24)

    def lay(values):
        if xp is jnp:
            values = values.astype(BF16)
        rows = []
        for p in range(2):
            for m in range(M_DEV):
                pick = (here & (col % 8 == 2 * m + p)).astype(values.dtype)
                rows.append(xp.matmul(values[m], pick).reshape(chunks, 1, CHUNK, devices * BLK))
        return xp.concatenate(rows, axis=1).reshape(chunks, 2 * M_DEV * CHUNK, devices * BLK)

    return lay(table * quad[None, None, :]), lay(table).transpose(0, 2, 1)


def constants(devices, lon):
    modes = M_DEV * devices
    angle = (np.arange(modes)[:, None] * np.arange(lon)[None, :] % lon) * (2.0 * math.pi / lon)
    factor = np.where(np.arange(modes) == 0, 1.0, 2.0)[:, None]

    def pad(re, im):
        paired = np.stack([re, im], axis=1).reshape(devices, 2 * M_DEV, lon)
        return np.pad(paired, ((0, 0), (0, 2), (0, 0))).reshape(devices * 8, lon)

    bf = ml_dtypes.bfloat16
    fwd = pad(np.cos(angle) / lon, -np.sin(angle) / lon).astype(np.float32).astype(bf)
    inv = pad(factor * np.cos(angle), -factor * np.sin(angle)).T.astype(np.float32).astype(bf)
    return fwd, inv


def toeplitz(f_ref, b_ref, cycle, offset, slot):
    which = (cycle * 3 + offset) * 2 + slot
    odd = lax.rem(b_ref[which], 2)
    shape = (ROWS, WIN)
    delta = (
        lax.broadcasted_iota(jnp.int32, shape, 0)
        - lax.broadcasted_iota(jnp.int32, shape, 1)
        + (16 - 8 * odd)
    )
    parts = [jnp.zeros(shape, F32) for _ in range(KB)]
    for t in range(SB):
        hit = delta == t
        for k in range(KB):
            parts[k] = jnp.where(hit, f_ref[(which * SB + t) * KB + k], parts[k])
    return [part.astype(BF16) for part in parts]


def window_start(b_ref, cycle, offset, slot, first, lon):
    half = b_ref[(cycle * 3 + offset) * 2 + slot] // 2
    start = first + lon - 16 - 16 * half
    start = jnp.where(start >= lon, start - lon, start)
    return pl.multiple_of(start, 16)


def mix_tile(basis, mix_ref):
    basis = basis.astype(BF16)
    wide = jnp.concatenate([basis[k * ROWS : (k + 1) * ROWS] for k in range(KB)], axis=1)
    return jnp.dot(wide, mix_ref[...], preferred_element_type=F32)


def fill_toeplitz(t_ref, f_ref, b_ref, cycle, offset, column):
    for slot in range(2):
        parts = toeplitz(f_ref, b_ref, cycle, offset, slot)
        for k in range(KB):
            t_ref[k * ROWS : (k + 1) * ROWS, (column + slot) * WIN : (column + slot + 1) * WIN] = parts[k]


def inner_kernel(f_ref, b_ref, x_ref, mix_ref, fwd_ref, loc_ref, part_ref, th_ref, spec_ref, ext, t0, t1, t2):
    lon = x_ref.shape[1]
    for i in range(3):
        ext[i, 0:lon] = x_ref[i]
        ext[i, lon : lon + WIN] = x_ref[i, 0:WIN]
    plan = {0: ((0, 1), (1, 2)), 1: ((0, 0), (1, 1), (2, 2)), 2: ((1, 0), (2, 1))}
    tables = (t0, t1, t2)
    for i in range(3):
        for n, (_, offset) in enumerate(plan[i]):
            fill_toeplitz(tables[i], f_ref, b_ref, i, offset, 2 * n)
    fill_toeplitz(th_ref.at[0], f_ref, b_ref, 0, 0, 0)
    fill_toeplitz(th_ref.at[1], f_ref, b_ref, 2, 2, 0)

    def tile(a, carry):
        first = pl.multiple_of(a * ROWS, 16)
        for i in range(3):
            pieces = []
            for source, offset in plan[i]:
                for slot in range(2):
                    start = window_start(b_ref, i, offset, slot, first, lon)
                    pieces.append(ext[source, pl.ds(start, WIN), :])
            basis = jnp.dot(tables[i][...], jnp.concatenate(pieces, axis=0), preferred_element_type=F32)
            out = mix_tile(basis, mix_ref)
            if i == 1:
                loc_ref[pl.ds(first, ROWS), :] = out.astype(BF16)
            else:
                part_ref[i // 2, pl.ds(first, ROWS), :] = out
        return carry

    lax.fori_loop(0, lon // ROWS, tile, 0)
    spec_ref[...] = jnp.dot(fwd_ref[...], loc_ref[...], preferred_element_type=F32)


def outer_kernel(b_ref, north_ref, south_ref, th_ref, part_ref, spec_ref, mix_ref, fwd_ref, loc_ref, x_ref, ext):
    lon = north_ref.shape[0]
    for h, ref in enumerate((north_ref, south_ref)):
        ext[h, 0:lon] = ref[...]
        ext[h, lon : lon + WIN] = ref[0:WIN]

    def tile(a, carry):
        first = pl.multiple_of(a * ROWS, 16)
        for h in range(2):
            pieces = []
            for slot in range(2):
                start = window_start(b_ref, 2 * h, 2 * h, slot, first, lon)
                pieces.append(ext[h, pl.ds(start, WIN), :])
            basis = jnp.dot(th_ref[h], jnp.concatenate(pieces, axis=0), preferred_element_type=F32)
            out = mix_tile(basis, mix_ref) + part_ref[h, pl.ds(first, ROWS), :]
            loc_ref[h, pl.ds(first, ROWS), :] = out.astype(BF16)
        return carry

    lax.fori_loop(0, lon // ROWS, tile, 0)
    s0 = jnp.dot(fwd_ref[...], loc_ref[0], preferred_element_type=F32)
    s2 = jnp.dot(fwd_ref[...], loc_ref[1], preferred_element_type=F32)
    devices = x_ref.shape[0]
    three = [s.reshape(devices, 8, s.shape[1]) for s in (s0, spec_ref[...], s2)]
    three.append(jnp.zeros_like(three[0]))
    x_ref[...] = jnp.concatenate(three, axis=1).astype(BF16)


def spectral_kernel(
    devices, x_ref, ana_hbm, syn_hbm, gain_ref, w_ref, out_ref,
    recv, back, ret, ana, syn, wide, acc, load_sem, send_a, recv_a, send_b, recv_b,
):
    me = lax.axis_index("lat")
    chunks = ana_hbm.shape[1]
    mine = me if ana_hbm.shape[0] > 1 else 0
    width = w_ref.shape[1]
    half = M_DEV * CHUNK

    def load(ch):
        return (
            pltpu.make_async_copy(ana_hbm.at[mine, ch], ana, load_sem.at[0]),
            pltpu.make_async_copy(syn_hbm.at[mine, ch], syn, load_sem.at[1]),
        )

    for c in load(0):
        c.start()
    barrier = pltpu.get_barrier_semaphore()

    def greet(s, carry):
        pl.semaphore_signal(barrier, inc=1, device_id={"lat": lax.rem(me + s, devices)}, device_id_type=MESH)
        return carry

    lax.fori_loop(1, devices, greet, 0)
    pl.semaphore_wait(barrier, devices - 1)

    def remote(src, dst, ssem, rsem, s, to, row):
        return pltpu.make_async_remote_copy(
            src_ref=src.at[to], dst_ref=dst.at[row], send_sem=ssem.at[s], recv_sem=rsem.at[row],
            device_id={"lat": to}, device_id_type=MESH,
        )

    def start_all(src, dst, ssem, rsem):
        def one(s, carry):
            remote(src, dst, ssem, rsem, s, lax.rem(me + s, devices), me).start()
            return carry

        lax.fori_loop(1, devices, one, 0)
        dst[me] = src[me]

    def wait_all(src, dst, ssem, rsem, send):
        def one(s, carry):
            peer = lax.rem(me + s, devices)
            copy = remote(src, dst, ssem, rsem, s, peer, peer)
            if send:
                copy.wait_send()
            else:
                copy.wait_recv()
            return carry

        lax.fori_loop(1, devices, one, 0)

    start_all(x_ref, recv, send_a, recv_a)
    wide[0:width, 0:width] = w_ref[0]
    wide[0:width, width:] = w_ref[1]
    wide[width:, 0:width] = -w_ref[1]
    wide[width:, width:] = w_ref[0]
    acc[...] = jnp.zeros_like(acc)
    wait_all(x_ref, recv, send_a, recv_a, False)

    rows = 16 * BLK

    def chunk(ch, carry):
        for c in load(ch):
            c.wait()
        data = recv[...].reshape(devices * BLK, width)
        coef = jnp.dot(ana[...], data, preferred_element_type=F32)
        gain = gain_ref[pl.ds(pl.multiple_of(ch * CHUNK, CHUNK), CHUNK), :]
        gain = jnp.concatenate([gain] * M_DEV, axis=0)
        scaled = jnp.concatenate([coef[:half] * gain, coef[half:] * gain], axis=1).astype(BF16)
        mixed = jnp.dot(scaled, wide[...], preferred_element_type=F32).astype(BF16)
        stacked = jnp.concatenate([mixed[:, :width], mixed[:, width:]], axis=0)

        def piece(r, inner):
            at = pl.ds(pl.multiple_of(r * rows, rows), rows)
            acc[at, :] += jnp.dot(syn[at, :], stacked, preferred_element_type=F32)
            return inner

        lax.fori_loop(0, devices * BLK // rows, piece, 0)

        @pl.when(ch + 1 < chunks)
        def _():
            for c in load(ch + 1):
                c.start()

        return carry

    lax.fori_loop(0, chunks, chunk, 0)
    back[...] = acc[...].reshape(devices, BLK, width).astype(BF16)
    start_all(back, ret, send_b, recv_b)
    wait_all(x_ref, recv, send_a, recv_a, True)
    wait_all(back, ret, send_b, recv_b, False)
    got = ret[...].astype(F32)
    for i in range(3):
        out_ref[i] = got[:, 8 * i : 8 * i + 8, :].reshape(devices * 8, width).astype(BF16)
    wait_all(back, ret, send_b, recv_b, True)


def final_kernel(mid_ref, edge_ref, modes_ref, inv_ref, out_ref):
    part = jnp.dot(inv_ref[...], modes_ref[0], preferred_element_type=F32)
    local = jnp.where(pl.program_id(0) == 1, mid_ref[...], edge_ref[0])
    out_ref[0] = jax.nn.gelu(local.astype(F32) + part).astype(BF16)


def body(devices, fwd_np, inv_np, leg_np, state, filters, blocks, mix, gain, weight):
    cycles, lon, ch = state.shape
    lat_count = cycles * devices
    chunks = lat_count // CHUNK
    fwd, inv = jnp.asarray(fwd_np), jnp.asarray(inv_np)
    up = [(i, i + 1) for i in range(devices - 1)]
    down = [(i + 1, i) for i in range(devices - 1)]
    north = lax.ppermute(state[cycles - 1], "lat", up)
    south = lax.ppermute(state[0], "lat", down)
    if leg_np is not None:
        ana, syn = jnp.asarray(leg_np[0]), jnp.asarray(leg_np[1])
    else:
        own = lax.axis_index("lat") * M_DEV + jnp.arange(M_DEV, dtype=jnp.int32)
        theta = (jnp.arange(lat_count, dtype=F32) + 0.5) * (math.pi / lat_count)
        quad = jnp.sin(theta) * (2.0 * math.pi * math.pi / lat_count)
        ana, syn = spread(jnp, legendre_table(own, lat_count, lat_count), quad, devices)
        ana, syn = ana.astype(BF16)[None], syn.astype(BF16)[None]

    vmem = pl.BlockSpec(memory_space=pltpu.VMEM)
    smem = pl.BlockSpec(memory_space=pltpu.SMEM)
    hbm = pl.BlockSpec(memory_space=pl.ANY)
    shape = jax.ShapeDtypeStruct
    fl, bl = filters.reshape(-1), blocks.reshape(-1)
    params = functools.partial(pltpu.CompilerParams, vmem_limit_bytes=48 * 2**20)
    loc1, part, th, spec1 = pl.pallas_call(
        inner_kernel,
        out_shape=(
            shape((lon, ch), BF16),
            shape((2, lon, ch), F32),
            shape((2, KB * ROWS, 2 * WIN), BF16),
            shape((devices * 8, ch), F32),
        ),
        in_specs=[smem, smem, vmem, vmem, vmem],
        out_specs=(vmem,) * 4,
        scratch_shapes=[
            pltpu.VMEM((3, lon + WIN, ch), BF16),
            pltpu.VMEM((KB * ROWS, 4 * WIN), BF16),
            pltpu.VMEM((KB * ROWS, 6 * WIN), BF16),
            pltpu.VMEM((KB * ROWS, 4 * WIN), BF16),
        ],
        compiler_params=params(),
        cost_estimate=pl.CostEstimate(flops=10**10, bytes_accessed=10**7, transcendentals=0),
        name="inner",
    )(fl, bl, state, mix, fwd)
    edges, xbuf = pl.pallas_call(
        outer_kernel,
        out_shape=(shape((2, lon, ch), BF16), shape((devices, BLK, ch), BF16)),
        in_specs=[smem] + [vmem] * 7,
        out_specs=(vmem, vmem),
        scratch_shapes=[pltpu.VMEM((2, lon + WIN, ch), BF16)],
        compiler_params=params(),
        name="outer",
    )(bl, north, south, th, part, spec1, mix, fwd)
    block = pltpu.VMEM((devices, BLK, ch), BF16)
    rows = 2 * M_DEV * CHUNK
    sems = pltpu.SemaphoreType.DMA((devices,))
    modes = pl.pallas_call(
        functools.partial(spectral_kernel, devices),
        out_shape=shape((3, devices * 8, ch), BF16),
        in_specs=[vmem, hbm, hbm, vmem, vmem],
        out_specs=vmem,
        scratch_shapes=[
            block, block, block,
            pltpu.VMEM((rows, devices * BLK), BF16),
            pltpu.VMEM((devices * BLK, rows), BF16),
            pltpu.VMEM((2 * ch, 2 * ch), BF16),
            pltpu.VMEM((devices * BLK, ch), F32),
            pltpu.SemaphoreType.DMA((2,)),
            sems, sems, sems, sems,
        ],
        compiler_params=params(collective_id=0, has_side_effects=True),
        name="spectral",
    )(xbuf, ana, syn, gain, weight)
    step = 480
    return pl.pallas_call(
        final_kernel,
        grid=(3, lon // step),
        out_shape=shape((cycles, lon, ch), BF16),
        in_specs=[
            pl.BlockSpec((step, ch), lambda i, n: (jnp.where(i == 1, n, jnp.where(i == 0, 0, lon // step - 1)), 0)),
            pl.BlockSpec((1, step, ch), lambda i, n: (i // 2, jnp.where(i == 1, lon // step - 1, n), 0)),
            pl.BlockSpec((1, devices * 8, ch), lambda i, n: (i, 0, 0)),
            pl.BlockSpec((step, devices * 8), lambda i, n: (n, 0)),
        ],
        out_specs=pl.BlockSpec((1, step, ch), lambda i, n: (i, n, 0)),
        compiler_params=params(),
        name="final",
    )(loc1, edges, modes, inv)


def solution(mesh):
    devices = mesh.shape["lat"]
    lon = 1440
    fwd, inv = constants(devices, lon)
    count = M_DEV * devices
    leg = None
    if count <= 96:
        table = legendre_np(count)
        quad = np.sin((np.arange(count) + 0.5) * (math.pi / count)) * (2.0 * math.pi**2 / count)
        pairs = [spread(np, table[M_DEV * d : M_DEV * d + M_DEV], quad, devices) for d in range(devices)]
        leg = [np.stack([p[n] for p in pairs]).astype(np.float32).astype(ml_dtypes.bfloat16) for n in range(2)]
    return jax.shard_map(
        functools.partial(body, devices, fwd, inv, leg),
        mesh=mesh,
        in_specs=(
            P(("groups", "lat"), None, None),
            P("lat", None, None, None, None),
            P("lat", None, None),
            P(),
            P(),
            P(),
        ),
        out_specs=P(("groups", "lat"), None, None),
        check_vma=False,
    )
```

time: 470 us -> 66.4 us (0.14); the launches traced: 462 us -> 65.2 us
  local copies, waits for them, and re-layouts: 191 us -> 6.03 us
  other arithmetic: 96.9 us -> 0.01 us
  loops' own time: 96 us -> 0 us
  Pallas kernels: 0 us -> 52.5 us
  matrix products: 51.6 us -> 0 us
  starting transfers between devices: 18.1 us -> 6.45 us
  waiting for transfers between devices: 8.5 us -> 0.01 us
    another operation x9 -> x0, loops' own time: 96 us -> none  [the longest x1 89.8 us: legendre_table(): lax.scan(advance, (zeros_state, zeros_state), degrees, unroll=16)]
    gather x54 -> x0, local copies, waits for them, and re-layouts: 82 us -> none
    pallas_call x0 -> x4, Pallas kernels: none -> 52.5 us  [the longest x1 20.4 us: body(): pl.pallas_call(inner_kernel, out_shape=(shape((lon, ch), BF16), shape((2,...]
    dot_general x18 -> x0, matrix products: 51.6 us -> none  [the longest x3 36.7 us: one_cycle(): jnp.einsum('avc,vw->awc', windows, table, precision=lax.Precision.HIGHEST)]
    eq x48 -> x0, other arithmetic: 29.9 us -> none  [the longest x24 15.6 us: advance(): degree == orders]
    lt x24 -> x0, other arithmetic: 29.7 us -> none  [advance(): degree < orders]
    slice x7 -> x0, local copies, waits for them, and re-layouts: 26.7 us -> none  [the longest x3 21.9 us: one_window(): return jnp.concatenate([piece[:-1], piece[1:]], axis=1)]
    convert_element_type x8 -> x0, local copies, waits for them, and re-layouts: 22.6 us -> none  [the longest x1 14.4 us: body(): summed.reshape(cycle_count, lon_count, KB * channels).astype(jnp.bfloat16)]
  transfers between devices with their start and end apart: 4 -> 2, of which waited for: 2 -> 0; matrix products, arithmetic and copies ran while one was open for 17% -> 2% of each run, Pallas kernels for 0% -> 31%
where the time goes in v1:
time: 66.4 us; the launch traced here: 65.2 us
  Pallas kernels  52.5 us (79%)
  starting transfers between devices  6.45 us (10%)
  local copies, waits for them, and re-layouts  6.03 us (9%)
    pallas_call x1, Pallas kernels, body(): pl.pallas_call(inner_kernel, out_shape=(shape((lon, ch), BF16), shape((2,...  20.4 us
    pallas_call x1, Pallas kernels, body(): pl.pallas_call(functools.partial(spectral_kernel, devices), out_shape=sha...  17.4 us
    pallas_call x1, Pallas kernels, body(): pl.pallas_call(outer_kernel, out_shape=(shape((2, lon, ch), BF16), shape(...  9.45 us
    pallas_call x1, Pallas kernels, body(): pl.pallas_call(final_kernel, grid=(3, lon // step), out_shape=shape((cycl...  5.21 us
    ppermute x1, starting transfers between devices, body(): north = lax.ppermute(state[cycles - 1], 'lat', up)  3.88 us
    unnamed x22, local copies, waits for them, and re-layouts  3.05 us
    squeeze x1, local copies, waits for them, and re-layouts, body(): south = lax.ppermute(state[0], 'lat', down)  2.69 us
    ppermute x1, starting transfers between devices, body(): south = lax.ppermute(state[0], 'lat', down)  2.57 us
  transfers between devices with their start and end apart: 2, of which 0 were waited for; matrix products, arithmetic and copies ran while one was open for 2% of the time, Pallas kernels for 31%

profile of v1, /device:TPU:13, one launch (start us, length us, event | category | flops | bytes accessed | tf_op | source)
XLA Modules:
  0.0 65.2 jit_solution(16835702661283818246)
XLA Ops:
  0.0 2.7 %slice_bitcast_fusion = (bf16[1440,256]{1,0:T(8,128)(2,1)}, bf16[1440,256]{1,0:T(8,128)(2,1)}) fusion(bf16[3,1440,256]{2,1,0:T(8,128)(2,1)} %x_ref.1), kind=kLoop, calls=%fused_computation | loop fusion | bytes 2949120 | tf_op jit(solution)/shard_map/squeeze | solution.py:330
  2.7 2.6 %collective-permute-start.1 = (bf16[1440,256]{1,0:T(8,128)(2,1)}, bf16[1440,256]{1,0:T(8,128)(2,1)S(1)}, u32[]{:S(2)}, u32[]{:S(2)}) collective-permute-start(bf16[1440,256]{1,0:T(8,128)(2,1)} %get-tuple-element.17), channel_id=1, source_target_pairs={{1,0},{2,1},{3,2},{4,3},{5,4},{6,5},{7,6},{8,7},{9,8},{10,9},{11,1... | collective-permute-start | bytes 2211848 | tf_op jit(solution)/shard_map/ppermute | solution.py:330
  5.3 3.9 %collective-permute-start = (bf16[1440,256]{1,0:T(8,128)(2,1)}, bf16[1440,256]{1,0:T(8,128)(2,1)}, u32[]{:S(2)}, u32[]{:S(2)}) collective-permute-start(bf16[1440,256]{1,0:T(8,128)(2,1)} %get-tuple-element.18), channel_id=1, source_target_pairs={{0,1},{1,2},{2,3},{3,4},{4,5},{5,6},{6,7},{7,8},{8,9},{9,10},{10,1... | collective-permute-start | bytes 2211848 | tf_op jit(solution)/shard_map/ppermute | solution.py:329
  9.2 0.0 copy-done.7
  9.2 0.1 copy.13
  9.3 0.1 reshape.7.b_ref
  9.4 0.9 %copy.12 = f32[3,3,2,8,3]{4,3,2,1,0:T(8,128)S(1)} copy(f32[3,3,2,8,3]{3,2,4,1,0:T(2,128)} %param.11) | data formatting | bytes 3456 | tf_op args[1]
  10.3 0.2 reshape.6.f_ref
  10.5 0.0 copy-done
  10.5 0.0 copy-start.1
  10.5 1.0 %copy-done.1 = bf16[768,256]{1,0:T(8,128)(2,1)S(1)} copy-done((bf16[768,256]{1,0:T(8,128)(2,1)S(1)}, bf16[768,256]{1,0:T(8,128)(2,1)}, u32[]{:S(2)}) %copy-start.1) | copy-done | bytes 393240
  11.5 1.0 %copy-done.3 = bf16[128,1440]{1,0:T(8,128)(2,1)S(1)} copy-done((bf16[128,1440]{1,0:T(8,128)(2,1)S(1)}, bf16[128,1440]{1,0:T(8,128)(2,1)}, u32[]{:S(2)}) %copy-start.3) | copy-done | bytes 368664
  12.5 20.4 %inner.1 = (bf16[1440,256]{1,0:T(8,128)(2,1)S(1)}, f32[2,1440,256]{2,1,0:T(8,128)}, bf16[2,288,256]{2,1,0:T(8,128)(2,1)S(1)}, f32[128,256]{1,0:T(8,128)S(1)}) custom-call(f32[432]{0:T(512)S(1)} %reshape.6.f_ref, s32[18]{0:T(128)S(1)} %reshape.7.b_ref, bf16[3,1440,256]{2,1,0:T(8,128)(2,1)S(1)} %copy-done, bf16[768,256]{1,0:T(8,128)(2,1)S(1)} %copy-done.1, ...), custom_call_target="tpu_custom_call" | custom-call | flops 10000000000 | bytes 10000000 | tf_op jit(solution)/shard_map/inner/pallas_call | solution.py:346
  33.0 0.0 collective-permute-done.1.south_ref
  33.0 0.0 collective-permute-done.north_ref
  33.0 0.0 copy-done.2
  33.0 0.0 copy-start.5
  33.0 0.0 copy-start.6
  33.0 9.5 %outer.1 = (bf16[2,1440,256]{2,1,0:T(8,128)(2,1)S(1)}, bf16[16,32,256]{2,1,0:T(8,128)(2,1)S(1)}) custom-call(s32[18]{0:T(128)S(1)} %reshape.7.b_ref, bf16[1440,256]{1,0:T(8,128)(2,1)} %collective-permute-done.north_ref, bf16[1440,256]{1,0:T(8,128)(2,1)S(1)} %collective-permute-done.1.south_ref, bf16[2,288,256]{2,1,0:T(8,128)(2,1)S(1)} %get-tuple-element.12.th_ref, ...), custom_call_target="tpu_custom_call" | custom-call | tf_op jit(solution)/shard_map/outer/pallas_call | solution.py:366
  42.5 0.0 slice-done
  42.5 0.0 copy-start.4
  42.5 17.4 %spectral.1.modes_ref = bf16[3,128,256]{2,1,0:T(8,128)(2,1)S(1)} custom-call(bf16[16,32,256]{2,1,0:T(8,128)(2,1)S(1)} %get-tuple-element.16.x_ref, bf16[16,1,288,512]{3,2,1,0:T(8,128)(2,1)S(1)} %bitcast.7, bf16[16,1,512,288]{3,2,1,0:T(8,128)(2,1)} %constant.11.clone.syn_hbm, f32[48,256]{1,0:T(8,128)S(1)} %copy-done.6, bf16[2,256,256]{2,1,0:T(8,128)(2,1)S(1)} %copy-done.5), custom_call_target="tpu_custom_call" | custom-call | tf_op jit(solution)/shard_map/spectral/pallas_call | solution.py:378
  59.9 0.0 copy-done.4
  59.9 5.2 %final.1 = bf16[3,1440,256]{2,1,0:T(8,128)(2,1)} custom-call(bf16[1440,256]{1,0:T(8,128)(2,1)S(1)} %get-tuple-element.11.mid_ref, bf16[2,1440,256]{2,1,0:T(8,128)(2,1)S(1)} %get-tuple-element.15.edge_ref, bf16[3,128,256]{2,1,0:T(8,128)(2,1)S(1)} %spectral.1.modes_ref, bf16[1440,128]{1,0:T(8,128)(2,1)S(1)} %copy-done.4), custom_call_target="tpu_custom_call" | custom-call | tf_op jit(solution)/shard_map/final/pallas_call | solution.py:396
  (10 shorter events, 0.0 us)
Async XLA Ops:
  0.0 10.5 %copy-start = (bf16[3,1440,256]{2,1,0:T(8,128)(2,1)S(1)}, bf16[3,1440,256]{2,1,0:T(8,128)(2,1)}, u32[]{:S(2)}) copy-start(bf16[3,1440,256]{2,1,0:T(8,128)(2,1)} %x_ref.1) | copy-start | bytes 6635524
  0.0 9.2 %copy-start.7 = (s32[3,3,2]{1,2,0:T(2,128)S(1)}, s32[3,3,2]{1,2,0:T(2,128)}, u32[]{:S(2)}) copy-start(s32[3,3,2]{1,2,0:T(2,128)} %param.12) | copy-start | bytes 220
  0.0 42.4 %slice-start = ((s8[4718592]{0:T(1024)(128)(4,1)}), s8[524288]{0:T(1024)(128)(4,1)S(1)}, s32[]{:S(2)}) async-start(s8[4718592]{0:T(1024)(128)(4,1)} %bitcast.6), calls=%async_computation | async-start | bytes 1048576
  2.7 30.3 %collective-permute-start.1 = (bf16[1440,256]{1,0:T(8,128)(2,1)}, bf16[1440,256]{1,0:T(8,128)(2,1)S(1)}, u32[]{:S(2)}, u32[]{:S(2)}) collective-permute-start(bf16[1440,256]{1,0:T(8,128)(2,1)} %get-tuple-element.17), channel_id=1, source_target_pairs={{1,0},{2,1},{3,2},{4,3},{5,4},{6,5},{7,6},{8,7},{9,8},{10,9},{11,1... | collective-permute-start | bytes 2211848 | tf_op jit(solution)/shard_map/ppermute | solution.py:330
  5.3 27.7 %collective-permute-start = (bf16[1440,256]{1,0:T(8,128)(2,1)}, bf16[1440,256]{1,0:T(8,128)(2,1)}, u32[]{:S(2)}, u32[]{:S(2)}) collective-permute-start(bf16[1440,256]{1,0:T(8,128)(2,1)} %get-tuple-element.18), channel_id=1, source_target_pairs={{0,1},{1,2},{2,3},{3,4},{4,5},{5,6},{6,7},{7,8},{8,9},{9,10},{10,1... | collective-permute-start | bytes 2211848 | tf_op jit(solution)/shard_map/ppermute | solution.py:329
  10.5 1.0 %copy-start.1 = (bf16[768,256]{1,0:T(8,128)(2,1)S(1)}, bf16[768,256]{1,0:T(8,128)(2,1)}, u32[]{:S(2)}) copy-start(bf16[768,256]{1,0:T(8,128)(2,1)} %mix_ref.3) | copy-start | bytes 1179652
  11.5 1.0 %copy-start.3 = (bf16[128,1440]{1,0:T(8,128)(2,1)S(1)}, bf16[128,1440]{1,0:T(8,128)(2,1)}, u32[]{:S(2)}) copy-start(bf16[128,1440]{1,0:T(8,128)(2,1)} %constant.8.clone.fwd_ref) | copy-start | bytes 1105924
  12.5 20.5 %copy-start.2 = (bf16[768,256]{1,0:T(8,128)(2,1)S(1)}, bf16[768,256]{1,0:T(8,128)(2,1)}, u32[]{:S(2)}) copy-start(bf16[768,256]{1,0:T(8,128)(2,1)} %mix_ref.3) | copy-start | bytes 1179652
  12.5 30.0 %slice-start.1 = ((s8[4718592]{0:T(1024)(128)(4,1)}), s8[4194304]{0:T(1024)(128)(4,1)S(1)}, s32[]{:S(2)}) async-start(s8[4718592]{0:T(1024)(128)(4,1)} %bitcast.6), calls=%async_computation.1 | async-start | bytes 8388608
  33.0 9.5 %copy-start.5 = (bf16[2,256,256]{2,1,0:T(8,128)(2,1)S(1)}, bf16[2,256,256]{2,1,0:T(8,128)(2,1)}, u32[]{:S(2)}) copy-start(bf16[2,256,256]{2,1,0:T(8,128)(2,1)} %w_ref.1) | copy-start | bytes 786436
  33.0 9.5 %copy-start.6 = (f32[48,256]{1,0:T(8,128)S(1)}, f32[48,256]{1,0:T(8,128)}, u32[]{:S(2)}) copy-start(f32[48,256]{1,0:T(8,128)} %gain_ref.1) | copy-start | bytes 147460
  42.5 17.4 %copy-start.4 = (bf16[1440,128]{1,0:T(8,128)(2,1)S(1)}, bf16[1440,128]{1,0:T(8,128)(2,1)}, u32[]{:S(2)}) copy-start(bf16[1440,128]{1,0:T(8,128)(2,1)} %constant.9.clone.inv_ref) | copy-start | bytes 1105924

commit v2 on v1

--- a/solution.py
+++ b/solution.py
@@ -13,8 +13,8 @@
 M_DEV = 3
 KB = 3
 SB = 8
-ROWS = 96
-WIN = 128
+ROWS = 48
+WIN = 64
 CHUNK = 48
 BLK = 32
 log_cut = -69.0
@@ -117,112 +117,66 @@
     return fwd, inv
 
 
-def toeplitz(f_ref, b_ref, cycle, offset, slot):
-    which = (cycle * 3 + offset) * 2 + slot
-    odd = lax.rem(b_ref[which], 2)
-    shape = (ROWS, WIN)
+def fill_toeplitz(t_ref, f_ref, o_ref, cycle, offset, column):
+    shape = (ROWS, 2 * WIN)
+    lane = lax.broadcasted_iota(jnp.int32, shape, 1)
+    first_slot = lane < WIN
+    off = [o_ref[cycle, slot, offset] for slot in range(2)]
     delta = (
         lax.broadcasted_iota(jnp.int32, shape, 0)
-        - lax.broadcasted_iota(jnp.int32, shape, 1)
-        + (16 - 8 * odd)
+        + jnp.where(first_slot, off[0], off[1] + WIN)
+        - lane
     )
     parts = [jnp.zeros(shape, F32) for _ in range(KB)]
     for t in range(SB):
         hit = delta == t
         for k in range(KB):
-            parts[k] = jnp.where(hit, f_ref[(which * SB + t) * KB + k], parts[k])
-    return [part.astype(BF16) for part in parts]
-
-
-def window_start(b_ref, cycle, offset, slot, first, lon):
-    half = b_ref[(cycle * 3 + offset) * 2 + slot] // 2
-    start = first + lon - 16 - 16 * half
-    start = jnp.where(start >= lon, start - lon, start)
-    return pl.multiple_of(start, 16)
-
-
-def mix_tile(basis, mix_ref):
-    basis = basis.astype(BF16)
-    wide = jnp.concatenate([basis[k * ROWS : (k + 1) * ROWS] for k in range(KB)], axis=1)
-    return jnp.dot(wide, mix_ref[...], preferred_element_type=F32)
-
-
-def fill_toeplitz(t_ref, f_ref, b_ref, cycle, offset, column):
+            value = jnp.where(first_slot, f_ref[cycle, offset, k, 0, t], f_ref[cycle, offset, k, 1, t])
+            parts[k] = jnp.where(hit, value, parts[k])
+    for k in range(KB):
+        t_ref[cycle, k * ROWS : (k + 1) * ROWS, column * 2 * WIN : (column + 1) * 2 * WIN] = parts[k].astype(BF16)
+
+
+def windows(b_ref, ref, cycle, offset, a):
+    pieces = []
     for slot in range(2):
-        parts = toeplitz(f_ref, b_ref, cycle, offset, slot)
-        for k in range(KB):
-            t_ref[k * ROWS : (k + 1) * ROWS, (column + slot) * WIN : (column + slot + 1) * WIN] = parts[k]
-
-
-def inner_kernel(f_ref, b_ref, x_ref, mix_ref, fwd_ref, loc_ref, part_ref, th_ref, spec_ref, ext, t0, t1, t2):
-    lon = x_ref.shape[1]
-    for i in range(3):
-        ext[i, 0:lon] = x_ref[i]
-        ext[i, lon : lon + WIN] = x_ref[i, 0:WIN]
-    plan = {0: ((0, 1), (1, 2)), 1: ((0, 0), (1, 1), (2, 2)), 2: ((1, 0), (2, 1))}
-    tables = (t0, t1, t2)
-    for i in range(3):
-        for n, (_, offset) in enumerate(plan[i]):
-            fill_toeplitz(tables[i], f_ref, b_ref, i, offset, 2 * n)
-    fill_toeplitz(th_ref.at[0], f_ref, b_ref, 0, 0, 0)
-    fill_toeplitz(th_ref.at[1], f_ref, b_ref, 2, 2, 0)
-
-    def tile(a, carry):
-        first = pl.multiple_of(a * ROWS, 16)
-        for i in range(3):
-            pieces = []
-            for source, offset in plan[i]:
-                for slot in range(2):
-                    start = window_start(b_ref, i, offset, slot, first, lon)
-                    pieces.append(ext[source, pl.ds(start, WIN), :])
-            basis = jnp.dot(tables[i][...], jnp.concatenate(pieces, axis=0), preferred_element_type=F32)
-            out = mix_tile(basis, mix_ref)
-            if i == 1:
-                loc_ref[pl.ds(first, ROWS), :] = out.astype(BF16)
-            else:
-                part_ref[i // 2, pl.ds(first, ROWS), :] = out
-        return carry
-
-    lax.fori_loop(0, lon // ROWS, tile, 0)
-    spec_ref[...] = jnp.dot(fwd_ref[...], loc_ref[...], preferred_element_type=F32)
-
-
-def outer_kernel(b_ref, north_ref, south_ref, th_ref, part_ref, spec_ref, mix_ref, fwd_ref, loc_ref, x_ref, ext):
-    lon = north_ref.shape[0]
-    for h, ref in enumerate((north_ref, south_ref)):
-        ext[h, 0:lon] = ref[...]
-        ext[h, lon : lon + WIN] = ref[0:WIN]
-
-    def tile(a, carry):
-        first = pl.multiple_of(a * ROWS, 16)
-        for h in range(2):
-            pieces = []
-            for slot in range(2):
-                start = window_start(b_ref, 2 * h, 2 * h, slot, first, lon)
-                pieces.append(ext[h, pl.ds(start, WIN), :])
-            basis = jnp.dot(th_ref[h], jnp.concatenate(pieces, axis=0), preferred_element_type=F32)
-            out = mix_tile(basis, mix_ref) + part_ref[h, pl.ds(first, ROWS), :]
-            loc_ref[h, pl.ds(first, ROWS), :] = out.astype(BF16)
-        return carry
-
-    lax.fori_loop(0, lon // ROWS, tile, 0)
-    s0 = jnp.dot(fwd_ref[...], loc_ref[0], preferred_element_type=F32)
-    s2 = jnp.dot(fwd_ref[...], loc_ref[1], preferred_element_type=F32)
-    devices = x_ref.shape[0]
-    three = [s.reshape(devices, 8, s.shape[1]) for s in (s0, spec_ref[...], s2)]
-    three.append(jnp.zeros_like(three[0]))
-    x_ref[...] = jnp.concatenate(three, axis=1).astype(BF16)
-
-
-def spectral_kernel(
-    devices, x_ref, ana_hbm, syn_hbm, gain_ref, w_ref, out_ref,
-    recv, back, ret, ana, syn, wide, acc, load_sem, send_a, recv_a, send_b, recv_b,
+        row = b_ref[cycle, slot, offset] + a * (ROWS // 16)
+        pieces += [ref[row + n] for n in range(WIN // 16)]
+    return pieces
+
+
+def main_kernel(
+    devices, f_ref, b_ref, o_ref, x_hbm, mix_ref, fwd_ref, ana_hbm, syn_hbm, gain_ref, w_ref,
+    loc_ref, out_ref,
+    e0, e1, e2, north, south, tab, bas, part, spec1,
+    x_ref, recv, back, ret, ana, syn, wide, acc,
+    load_sem, x_sem, halo_send, halo_recv, send_a, recv_a, send_b, recv_b,
 ):
     me = lax.axis_index("lat")
+    tiles = x_hbm.shape[1]
+    lon = tiles * 16
     chunks = ana_hbm.shape[1]
     mine = me if ana_hbm.shape[0] > 1 else 0
     width = w_ref.shape[1]
     half = M_DEV * CHUNK
+
+    barrier = pltpu.get_barrier_semaphore()
+
+    def greet(s, carry):
+        pl.semaphore_signal(barrier, inc=1, device_id={"lat": lax.rem(me + s, devices)}, device_id_type=MESH)
+        return carry
+
+    lax.fori_loop(1, devices, greet, 0)
+
+    held = (e0, e1, e2)
+    fetches = []
+    for i in range(3):
+        fetches.append(pltpu.make_async_copy(x_hbm.at[i], held[i].at[pl.ds(0, tiles)], x_sem.at[2 * i]))
+        fetches.append(
+            pltpu.make_async_copy(x_hbm.at[i], held[i].at[pl.ds(tiles, tiles)], x_sem.at[2 * i + 1])
+        )
+    for c in fetches:
+        c.start()
 
     def load(ch):
         return (
@@ -232,14 +186,98 @@
 
     for c in load(0):
         c.start()
-    barrier = pltpu.get_barrier_semaphore()
-
-    def greet(s, carry):
-        pl.semaphore_signal(barrier, inc=1, device_id={"lat": lax.rem(me + s, devices)}, device_id_type=MESH)
+    pl.semaphore_wait(barrier, devices - 1)
+
+    send_up = pltpu.make_async_remote_copy(
+        src_ref=x_hbm.at[2], dst_ref=north.at[pl.ds(0, tiles)], send_sem=halo_send.at[0], recv_sem=halo_recv.at[0],
+        device_id={"lat": lax.rem(me + 1, devices)}, device_id_type=MESH,
+    )
+    send_down = pltpu.make_async_remote_copy(
+        src_ref=x_hbm.at[0], dst_ref=south.at[pl.ds(0, tiles)], send_sem=halo_send.at[1], recv_sem=halo_recv.at[1],
+        device_id={"lat": lax.rem(me + devices - 1, devices)}, device_id_type=MESH,
+    )
+
+    @pl.when(me < devices - 1)
+    def _():
+        send_up.start()
+
+    @pl.when(me > 0)
+    def _():
+        send_down.start()
+
+    plan = {0: ((0, 1), (1, 2)), 1: ((0, 0), (1, 1), (2, 2)), 2: ((1, 0), (2, 1))}
+    for i in range(3):
+        for n, (_, offset) in enumerate(plan[i]):
+            fill_toeplitz(tab, f_ref, o_ref, i, offset, n)
+    fill_toeplitz(tab, f_ref, o_ref, 0, 0, 2)
+    fill_toeplitz(tab, f_ref, o_ref, 2, 2, 2)
+    wide[0:width, 0:width] = w_ref[0]
+    wide[0:width, width:] = w_ref[1]
+    wide[width:, 0:width] = -w_ref[1]
+    wide[width:, width:] = w_ref[0]
+    acc[...] = jnp.zeros_like(acc)
+    for c in fetches:
+        c.wait()
+
+    def keep(i, first, basis):
+        basis = basis.astype(BF16)
+        for k in range(KB):
+            bas[i, pl.ds(first, ROWS), k * width : (k + 1) * width] = basis[k * ROWS : (k + 1) * ROWS]
+
+    def inner(a, carry):
+        first = pl.multiple_of(a * ROWS, 16)
+        for i in range(3):
+            pieces = []
+            for source, offset in plan[i]:
+                pieces += windows(b_ref, held[source], i, offset, a)
+            used = len(pieces) * 16
+            basis = jnp.dot(tab[i, :, 0:used], jnp.concatenate(pieces, axis=0), preferred_element_type=F32)
+            if i == 1:
+                keep(i, first, basis)
+            else:
+                part[i // 2, a] = basis
         return carry
 
-    lax.fori_loop(1, devices, greet, 0)
-    pl.semaphore_wait(barrier, devices - 1)
+    lax.fori_loop(0, lon // ROWS, inner, 0)
+
+    step = lon // 3
+
+    def mix_cycle(i):
+        def one(n, carry):
+            at = pl.ds(pl.multiple_of(n * step, 16), step)
+            loc_ref[i, at, :] = jnp.dot(bas[i, at, :], mix_ref[...], preferred_element_type=F32).astype(BF16)
+            return carry
+
+        lax.fori_loop(0, 3, one, 0)
+        return jnp.dot(fwd_ref[...], loc_ref[i], preferred_element_type=F32)
+
+    spec1[...] = mix_cycle(1)
+
+    for ref, inside, copy in ((north, me > 0, send_up), (south, me < devices - 1, send_down)):
+        @pl.when(inside)
+        def _(copy=copy):
+            copy.wait_recv()
+
+        @pl.when(jnp.logical_not(inside))
+        def _(ref=ref):
+            ref[0:tiles] = jnp.zeros((tiles, 16, width), BF16)
+
+        ref[tiles : 2 * tiles] = ref[0:tiles]
+
+    def outer(a, carry):
+        first = pl.multiple_of(a * ROWS, 16)
+        for h, ref in enumerate((north, south)):
+            pieces = windows(b_ref, ref, 2 * h, 2 * h, a)
+            basis = jnp.dot(tab[2 * h, :, 4 * WIN :], jnp.concatenate(pieces, axis=0), preferred_element_type=F32)
+            keep(2 * h, first, basis + part[h, a])
+        return carry
+
+    lax.fori_loop(0, lon // ROWS, outer, 0)
+    s0 = mix_cycle(0)
+    s2 = mix_cycle(2)
+    three = [s.reshape(devices, 8, width) for s in (s0, spec1[...], s2)]
+    three.append(jnp.zeros_like(three[0]))
+    x_ref[...] = jnp.concatenate(three, axis=1).astype(BF16)
 
     def remote(src, dst, ssem, rsem, s, to, row):
         return pltpu.make_async_remote_copy(
@@ -268,11 +306,15 @@
         lax.fori_loop(1, devices, one, 0)
 
     start_all(x_ref, recv, send_a, recv_a)
-    wide[0:width, 0:width] = w_ref[0]
-    wide[0:width, width:] = w_ref[1]
-    wide[width:, 0:width] = -w_ref[1]
-    wide[width:, width:] = w_ref[0]
-    acc[...] = jnp.zeros_like(acc)
+
+    @pl.when(me < devices - 1)
+    def _():
+        send_up.wait_send()
+
+    @pl.when(me > 0)
+    def _():
+        send_down.wait_send()
+
     wait_all(x_ref, recv, send_a, recv_a, False)
 
     rows = 16 * BLK
@@ -288,10 +330,10 @@
         mixed = jnp.dot(scaled, wide[...], preferred_element_type=F32).astype(BF16)
         stacked = jnp.concatenate([mixed[:, :width], mixed[:, width:]], axis=0)
 
-        def piece(r, inner):
+        def piece(r, inner_carry):
             at = pl.ds(pl.multiple_of(r * rows, rows), rows)
             acc[at, :] += jnp.dot(syn[at, :], stacked, preferred_element_type=F32)
-            return inner
+            return inner_carry
 
         lax.fori_loop(0, devices * BLK // rows, piece, 0)
 
@@ -313,21 +355,15 @@
     wait_all(back, ret, send_b, recv_b, True)
 
 
-def final_kernel(mid_ref, edge_ref, modes_ref, inv_ref, out_ref):
+def final_kernel(local_ref, modes_ref, inv_ref, out_ref):
     part = jnp.dot(inv_ref[...], modes_ref[0], preferred_element_type=F32)
-    local = jnp.where(pl.program_id(0) == 1, mid_ref[...], edge_ref[0])
-    out_ref[0] = jax.nn.gelu(local.astype(F32) + part).astype(BF16)
+    out_ref[0] = jax.nn.gelu(local_ref[0].astype(F32) + part).astype(BF16)
 
 
 def body(devices, fwd_np, inv_np, leg_np, state, filters, blocks, mix, gain, weight):
     cycles, lon, ch = state.shape
     lat_count = cycles * devices
-    chunks = lat_count // CHUNK
     fwd, inv = jnp.asarray(fwd_np), jnp.asarray(inv_np)
-    up = [(i, i + 1) for i in range(devices - 1)]
-    down = [(i + 1, i) for i in range(devices - 1)]
-    north = lax.ppermute(state[cycles - 1], "lat", up)
-    south = lax.ppermute(state[0], "lat", down)
     if leg_np is not None:
         ana, syn = jnp.asarray(leg_np[0]), jnp.asarray(leg_np[1])
     else:
@@ -341,72 +377,54 @@
     smem = pl.BlockSpec(memory_space=pltpu.SMEM)
     hbm = pl.BlockSpec(memory_space=pl.ANY)
     shape = jax.ShapeDtypeStruct
-    fl, bl = filters.reshape(-1), blocks.reshape(-1)
     params = functools.partial(pltpu.CompilerParams, vmem_limit_bytes=48 * 2**20)
-    loc1, part, th, spec1 = pl.pallas_call(
-        inner_kernel,
-        out_shape=(
-            shape((lon, ch), BF16),
-            shape((2, lon, ch), F32),
-            shape((2, KB * ROWS, 2 * WIN), BF16),
-            shape((devices * 8, ch), F32),
-        ),
-        in_specs=[smem, smem, vmem, vmem, vmem],
-        out_specs=(vmem,) * 4,
-        scratch_shapes=[
-            pltpu.VMEM((3, lon + WIN, ch), BF16),
-            pltpu.VMEM((KB * ROWS, 4 * WIN), BF16),
-            pltpu.VMEM((KB * ROWS, 6 * WIN), BF16),
-            pltpu.VMEM((KB * ROWS, 4 * WIN), BF16),
-        ],
-        compiler_params=params(),
-        cost_estimate=pl.CostEstimate(flops=10**10, bytes_accessed=10**7, transcendentals=0),
-        name="inner",
-    )(fl, bl, state, mix, fwd)
-    edges, xbuf = pl.pallas_call(
-        outer_kernel,
-        out_shape=(shape((2, lon, ch), BF16), shape((devices, BLK, ch), BF16)),
-        in_specs=[smem] + [vmem] * 7,
-        out_specs=(vmem, vmem),
-        scratch_shapes=[pltpu.VMEM((2, lon + WIN, ch), BF16)],
-        compiler_params=params(),
-        name="outer",
-    )(bl, north, south, th, part, spec1, mix, fwd)
     block = pltpu.VMEM((devices, BLK, ch), BF16)
+    cycle = pltpu.VMEM((lon // 8, 16, ch), BF16)
     rows = 2 * M_DEV * CHUNK
     sems = pltpu.SemaphoreType.DMA((devices,))
-    modes = pl.pallas_call(
-        functools.partial(spectral_kernel, devices),
-        out_shape=shape((3, devices * 8, ch), BF16),
-        in_specs=[vmem, hbm, hbm, vmem, vmem],
-        out_specs=vmem,
+    turned = jnp.transpose(blocks, (0, 2, 1))
+    local, modes = pl.pallas_call(
+        functools.partial(main_kernel, devices),
+        out_shape=(shape((cycles, lon, ch), BF16), shape((3, devices * 8, ch), BF16)),
+        in_specs=[smem, smem, smem, hbm, vmem, vmem, hbm, hbm, vmem, vmem],
+        out_specs=(vmem, vmem),
         scratch_shapes=[
-            block, block, block,
+            cycle, cycle, cycle, cycle, cycle,
+            pltpu.VMEM((3, KB * ROWS, 6 * WIN), BF16),
+            pltpu.VMEM((3, lon, KB * ch), BF16),
+            pltpu.VMEM((2, lon // ROWS, KB * ROWS, ch), F32),
+            pltpu.VMEM((devices * 8, ch), F32),
+            block, block, block, block,
             pltpu.VMEM((rows, devices * BLK), BF16),
             pltpu.VMEM((devices * BLK, rows), BF16),
             pltpu.VMEM((2 * ch, 2 * ch), BF16),
             pltpu.VMEM((devices * BLK, ch), F32),
             pltpu.SemaphoreType.DMA((2,)),
+            pltpu.SemaphoreType.DMA((6,)),
+            pltpu.SemaphoreType.DMA((2,)),
+            pltpu.SemaphoreType.DMA((2,)),
             sems, sems, sems, sems,
         ],
         compiler_params=params(collective_id=0, has_side_effects=True),
-        name="spectral",
-    )(xbuf, ana, syn, gain, weight)
+        name="main",
+    )(
+        jnp.transpose(filters, (0, 1, 4, 2, 3)), lon // 16 - 1 - turned // 2, 16 - 8 * (turned % 2),
+        state.reshape(cycles, lon // 16, 16, ch), mix, fwd, ana, syn, gain, weight,
+    )
     step = 480
     return pl.pallas_call(
         final_kernel,
         grid=(3, lon // step),
         out_shape=shape((cycles, lon, ch), BF16),
         in_specs=[
-            pl.BlockSpec((step, ch), lambda i, n: (jnp.where(i == 1, n, jnp.where(i == 0, 0, lon // step - 1)), 0)),
-            pl.BlockSpec((1, step, ch), lambda i, n: (i // 2, jnp.where(i == 1, lon // step - 1, n), 0)),
+            pl.BlockSpec((1, step, ch), lambda i, n: (i, n, 0)),
             pl.BlockSpec((1, devices * 8, ch), lambda i, n: (i, 0, 0)),
             pl.BlockSpec((step, devices * 8), lambda i, n: (n, 0)),
         ],
         out_specs=pl.BlockSpec((1, step, ch), lambda i, n: (i, n, 0)),
         compiler_params=params(),
         name="final",
-    )(loc1, edges, modes, inv)
+    )(local, modes, inv)
 
 
 def solution(mesh):

time: 66.4 us -> 57.5 us (0.87); the launches traced: 65.2 us -> 57.1 us
  starting transfers between devices: 6.45 us -> 0 us
  Pallas kernels: 52.5 us -> 50.2 us
  other arithmetic: 0.01 us -> 0.7 us
    ppermute x2 -> x0, starting transfers between devices: 6.45 us -> none  [the longest x1 3.88 us: body(): north = lax.ppermute(state[cycles - 1], 'lat', up)]
    unnamed x22 -> x14, local copies, waits for them, and re-layouts: 3.05 us -> 6.11 us
    squeeze x1 -> x0, local copies, waits for them, and re-layouts: 2.69 us -> none  [body(): south = lax.ppermute(state[0], 'lat', down)]
    pallas_call x3 -> x1, Pallas kernels: 47.3 us -> 45.1 us  [body(): pl.pallas_call(functools.partial(main_kernel, devices), out_shape=(shape(...]
    sub x0 -> x1, other arithmetic: none -> 0.7 us  [body(): 16 - 8 * (turned % 2)]
  transfers between devices with their start and end apart: 2 -> 0, of which waited for: 0 -> 0; matrix products, arithmetic and copies ran while one was open for 2% -> 0% of each run, Pallas kernels for 31% -> 0%
where the time goes in v2:
time: 57.5 us; the launch traced here: 57.1 us
  Pallas kernels  50.2 us (87%)
  local copies, waits for them, and re-layouts  6.11 us (11%)
  other arithmetic  0.7 us (1%)
    pallas_call x1, Pallas kernels, body(): pl.pallas_call(functools.partial(main_kernel, devices), out_shape=(shape(...  45.1 us
    unnamed x14, local copies, waits for them, and re-layouts  6.11 us
    pallas_call x1, Pallas kernels, body(): pl.pallas_call(final_kernel, grid=(3, lon // step), out_shape=shape((cycl...  5.17 us

profile of v2, /device:TPU:13, one launch (start us, length us, event | category | flops | bytes accessed | tf_op | source)
XLA Modules:
  0.0 57.1 jit_solution(8565967892472676387)
XLA Ops:
  0.0 0.7 %fusion.1 = (s32[3,2,3]{2,1,0:T(2,128)S(1)}, s32[3,2,3]{2,1,0:T(2,128)S(1)}) fusion(s32[3,3,2]{1,2,0:T(2,128)} %param.12), kind=kLoop, calls=%fused_computation.8 | loop fusion | flops 396 | bytes 216 | tf_op jit(solution)/shard_map/sub | solution.py:411
  0.7 0.0 copy-start
  0.7 1.6 %copy-done = bf16[3,1440,256]{2,1,0:T(8,128)(2,1)S(1)} copy-done((bf16[3,1440,256]{2,1,0:T(8,128)(2,1)S(1)}, bf16[3,1440,256]{2,1,0:T(8,128)(2,1)}, u32[]{:S(2)}) %copy-start) | copy-done | bytes 2211864
  2.3 0.0 copy-start.1
  2.3 1.0 %copy-done.1 = bf16[768,256]{1,0:T(8,128)(2,1)S(1)} copy-done((bf16[768,256]{1,0:T(8,128)(2,1)S(1)}, bf16[768,256]{1,0:T(8,128)(2,1)}, u32[]{:S(2)}) %copy-start.1) | copy-done | bytes 393240
  3.3 0.0 copy-start.2
  3.3 1.0 %copy-done.2 = bf16[128,1440]{1,0:T(8,128)(2,1)S(1)} copy-done((bf16[128,1440]{1,0:T(8,128)(2,1)S(1)}, bf16[128,1440]{1,0:T(8,128)(2,1)}, u32[]{:S(2)}) %copy-start.2) | copy-done | bytes 368664
  4.3 0.0 copy-start.4
  4.3 0.9 %copy-done.4 = bf16[2,256,256]{2,1,0:T(8,128)(2,1)S(1)} copy-done((bf16[2,256,256]{2,1,0:T(8,128)(2,1)S(1)}, bf16[2,256,256]{2,1,0:T(8,128)(2,1)}, u32[]{:S(2)}) %copy-start.4) | copy-done | bytes 262168
  5.3 0.0 copy-start.5
  5.3 0.8 %copy-done.5 = f32[48,256]{1,0:T(8,128)S(1)} copy-done((f32[48,256]{1,0:T(8,128)S(1)}, f32[48,256]{1,0:T(8,128)}, u32[]{:S(2)}) %copy-start.5) | copy-done | bytes 49176
  6.1 0.0 copy-start.6
  6.1 0.7 %copy-done.6 = f32[3,3,2,8,3]{3,2,4,1,0:T(2,128)S(1)} copy-done((f32[3,3,2,8,3]{3,2,4,1,0:T(2,128)S(1)}, f32[3,3,2,8,3]{3,2,4,1,0:T(2,128)}, u32[]{:S(2)}) %copy-start.6) | copy-done | bytes 1752
  6.8 0.0 copy-start.3
  6.8 45.1 %main.1 = (bf16[3,1440,256]{2,1,0:T(8,128)(2,1)S(1)}, bf16[3,128,256]{2,1,0:T(8,128)(2,1)S(1)}) custom-call(f32[3,3,3,2,8]{4,3,2,1,0:T(2,128)S(1)} %bitcast.25, s32[3,2,3]{2,1,0:T(2,128)S(1)} %get-tuple-element.10.b_ref, s32[3,2,3]{2,1,0:T(2,128)S(1)} %get-tuple-element.9.o_ref, bf16[3,90,16,256]{3,2,1,0:T(8,128)(2,1)S(1)} %bitcast.24, ...), custom_call_target="tpu_custom_call" | custom-call | tf_op jit(solution)/shard_map/main/pallas_call | solution.py:386
  51.9 0.0 copy-done.3
  51.9 5.2 %final.1 = bf16[3,1440,256]{2,1,0:T(8,128)(2,1)} custom-call(bf16[3,1440,256]{2,1,0:T(8,128)(2,1)S(1)} %get-tuple-element.7.local_ref, bf16[3,128,256]{2,1,0:T(8,128)(2,1)S(1)} %get-tuple-element.8.modes_ref, bf16[1440,128]{1,0:T(8,128)(2,1)S(1)} %copy-done.3), custom_call_target="tpu_custom_call" | custom-call | tf_op jit(solution)/shard_map/final/pallas_call | solution.py:415
Async XLA Ops:
  0.7 1.6 %copy-start = (bf16[3,1440,256]{2,1,0:T(8,128)(2,1)S(1)}, bf16[3,1440,256]{2,1,0:T(8,128)(2,1)}, u32[]{:S(2)}) copy-start(bf16[3,1440,256]{2,1,0:T(8,128)(2,1)} %param.10) | copy-start | bytes 6635524
  2.3 1.0 %copy-start.1 = (bf16[768,256]{1,0:T(8,128)(2,1)S(1)}, bf16[768,256]{1,0:T(8,128)(2,1)}, u32[]{:S(2)}) copy-start(bf16[768,256]{1,0:T(8,128)(2,1)} %mix_ref.1) | copy-start | bytes 1179652
  3.3 1.0 %copy-start.2 = (bf16[128,1440]{1,0:T(8,128)(2,1)S(1)}, bf16[128,1440]{1,0:T(8,128)(2,1)}, u32[]{:S(2)}) copy-start(bf16[128,1440]{1,0:T(8,128)(2,1)} %constant.40.clone.fwd_ref) | copy-start | bytes 1105924
  4.3 0.9 %copy-start.4 = (bf16[2,256,256]{2,1,0:T(8,128)(2,1)S(1)}, bf16[2,256,256]{2,1,0:T(8,128)(2,1)}, u32[]{:S(2)}) copy-start(bf16[2,256,256]{2,1,0:T(8,128)(2,1)} %w_ref.1) | copy-start | bytes 786436
  5.3 0.8 %copy-start.5 = (f32[48,256]{1,0:T(8,128)S(1)}, f32[48,256]{1,0:T(8,128)}, u32[]{:S(2)}) copy-start(f32[48,256]{1,0:T(8,128)} %gain_ref.1) | copy-start | bytes 147460
  6.1 0.7 %copy-start.6 = (f32[3,3,2,8,3]{3,2,4,1,0:T(2,128)S(1)}, f32[3,3,2,8,3]{3,2,4,1,0:T(2,128)}, u32[]{:S(2)}) copy-start(f32[3,3,2,8,3]{3,2,4,1,0:T(2,128)} %param.11) | copy-start | bytes 5188
  6.8 45.1 %copy-start.3 = (bf16[1440,128]{1,0:T(8,128)(2,1)S(1)}, bf16[1440,128]{1,0:T(8,128)(2,1)}, u32[]{:S(2)}) copy-start(bf16[1440,128]{1,0:T(8,128)(2,1)} %constant.41.clone.inv_ref) | copy-start | bytes 1105924

commit v3 on v2

--- a/solution.py
+++ b/solution.py
@@ -88,8 +88,12 @@
     lat = xp.arange(count)[:, None]
     col = xp.arange(devices * BLK)[None, :]
     here = (lat == 3 * (col // BLK) + col % BLK // 8) & (col % BLK < 24)
-
-    def lay(values):
+    per = devices * 16
+    late = col // per
+    source = xp.where(late == 0, 1, 2 * (col % 16 // 8))
+    there = (lat == 3 * (col % per // 16) + source) & ((late == 1) | (col % 16 < 8))
+
+    def lay(values, here):
         if xp is jnp:
             values = values.astype(BF16)
         rows = []
@@ -99,7 +103,7 @@
                 rows.append(xp.matmul(values[m], pick).reshape(chunks, 1, CHUNK, devices * BLK))
         return xp.concatenate(rows, axis=1).reshape(chunks, 2 * M_DEV * CHUNK, devices * BLK)
 
-    return lay(table * quad[None, None, :]), lay(table).transpose(0, 2, 1)
+    return lay(table * quad[None, None, :], there), lay(table, here).transpose(0, 2, 1)
 
 
 def constants(devices, lon):
@@ -146,18 +150,19 @@
 
 
 def main_kernel(
-    devices, f_ref, b_ref, o_ref, x_hbm, mix_ref, fwd_ref, ana_hbm, syn_hbm, gain_ref, w_ref,
-    loc_ref, out_ref,
-    e0, e1, e2, north, south, tab, bas, part, spec1,
-    x_ref, recv, back, ret, ana, syn, wide, acc,
-    load_sem, x_sem, halo_send, halo_recv, send_a, recv_a, send_b, recv_b,
+    devices, f_ref, b_ref, o_ref, x_hbm, mix_hbm, fwd_hbm, ana_hbm, syn_hbm, gain_hbm, w_hbm,
+    loc_hbm, out_ref,
+    loc_ref, mix_ref, fwd_ref, gain_ref, w_ref, own_sem, loc_sem,
+    e0, e1, e2, north, south, tab, bas, part,
+    x_mid, x_ref, recv_mid, recv, back, ret, ana, syn, wide, acc,
+    load_sem, x_sem, halo_send, halo_recv, send_a, recv_a, send_b, recv_b, send_c, recv_c,
 ):
     me = lax.axis_index("lat")
     tiles = x_hbm.shape[1]
     lon = tiles * 16
     chunks = ana_hbm.shape[1]
     mine = me if ana_hbm.shape[0] > 1 else 0
-    width = w_ref.shape[1]
+    width = w_ref.shape[2]
     half = M_DEV * CHUNK
 
     barrier = pltpu.get_barrier_semaphore()
@@ -177,6 +182,14 @@
         )
     for c in fetches:
         c.start()
+    small = [
+        pltpu.make_async_copy(src, dst, own_sem.at[n])
+        for n, (src, dst) in enumerate(
+            ((w_hbm, w_ref), (mix_hbm, mix_ref), (fwd_hbm, fwd_ref), (gain_hbm, gain_ref))
+        )
+    ]
+    for c in small:
+        c.start()
 
     def load(ch):
         return (
@@ -211,6 +224,8 @@
             fill_toeplitz(tab, f_ref, o_ref, i, offset, n)
     fill_toeplitz(tab, f_ref, o_ref, 0, 0, 2)
     fill_toeplitz(tab, f_ref, o_ref, 2, 2, 2)
+    for c in small:
+        c.wait()
     wide[0:width, 0:width] = w_ref[0]
     wide[0:width, width:] = w_ref[1]
     wide[width:, 0:width] = -w_ref[1]
@@ -240,45 +255,6 @@
 
     lax.fori_loop(0, lon // ROWS, inner, 0)
 
-    step = lon // 3
-
-    def mix_cycle(i):
-        def one(n, carry):
-            at = pl.ds(pl.multiple_of(n * step, 16), step)
-            loc_ref[i, at, :] = jnp.dot(bas[i, at, :], mix_ref[...], preferred_element_type=F32).astype(BF16)
-            return carry
-
-        lax.fori_loop(0, 3, one, 0)
-        return jnp.dot(fwd_ref[...], loc_ref[i], preferred_element_type=F32)
-
-    spec1[...] = mix_cycle(1)
-
-    for ref, inside, copy in ((north, me > 0, send_up), (south, me < devices - 1, send_down)):
-        @pl.when(inside)
-        def _(copy=copy):
-            copy.wait_recv()
-
-        @pl.when(jnp.logical_not(inside))
-        def _(ref=ref):
-            ref[0:tiles] = jnp.zeros((tiles, 16, width), BF16)
-
-        ref[tiles : 2 * tiles] = ref[0:tiles]
-
-    def outer(a, carry):
-        first = pl.multiple_of(a * ROWS, 16)
-        for h, ref in enumerate((north, south)):
-            pieces = windows(b_ref, ref, 2 * h, 2 * h, a)
-            basis = jnp.dot(tab[2 * h, :, 4 * WIN :], jnp.concatenate(pieces, axis=0), preferred_element_type=F32)
-            keep(2 * h, first, basis + part[h, a])
-        return carry
-
-    lax.fori_loop(0, lon // ROWS, outer, 0)
-    s0 = mix_cycle(0)
-    s2 = mix_cycle(2)
-    three = [s.reshape(devices, 8, width) for s in (s0, spec1[...], s2)]
-    three.append(jnp.zeros_like(three[0]))
-    x_ref[...] = jnp.concatenate(three, axis=1).astype(BF16)
-
     def remote(src, dst, ssem, rsem, s, to, row):
         return pltpu.make_async_remote_copy(
             src_ref=src.at[to], dst_ref=dst.at[row], send_sem=ssem.at[s], recv_sem=rsem.at[row],
@@ -305,6 +281,48 @@
 
         lax.fori_loop(1, devices, one, 0)
 
+    step = lon // 3
+
+    leave = [pltpu.make_async_copy(loc_ref.at[i], loc_hbm.at[i], loc_sem.at[i]) for i in range(3)]
+
+    def mix_cycle(i):
+        def one(n, carry):
+            at = pl.ds(pl.multiple_of(n * step, 16), step)
+            loc_ref[i, at, :] = jnp.dot(bas[i, at, :], mix_ref[...], preferred_element_type=F32).astype(BF16)
+            return carry
+
+        lax.fori_loop(0, 3, one, 0)
+        leave[i].start()
+        return jnp.dot(fwd_ref[...], loc_ref[i], preferred_element_type=F32)
+
+    mid = mix_cycle(1).reshape(devices, 8, width)
+    x_mid[...] = jnp.concatenate([mid, jnp.zeros_like(mid)], axis=1).astype(BF16)
+    start_all(x_mid, recv_mid, send_c, recv_c)
+
+    for ref, inside, copy in ((north, me > 0, send_up), (south, me < devices - 1, send_down)):
+        @pl.when(inside)
+        def _(copy=copy):
+            copy.wait_recv()
+
+        @pl.when(jnp.logical_not(inside))
+        def _(ref=ref):
+            ref[0:tiles] = jnp.zeros((tiles, 16, width), BF16)
+
+        ref[tiles : 2 * tiles] = ref[0:tiles]
+
+    def outer(a, carry):
+        first = pl.multiple_of(a * ROWS, 16)
+        for h, ref in enumerate((north, south)):
+            pieces = windows(b_ref, ref, 2 * h, 2 * h, a)
+            basis = jnp.dot(tab[2 * h, :, 4 * WIN :], jnp.concatenate(pieces, axis=0), preferred_element_type=F32)
+            keep(2 * h, first, basis + part[h, a])
+        return carry
+
+    lax.fori_loop(0, lon // ROWS, outer, 0)
+    s0 = mix_cycle(0)
+    s2 = mix_cycle(2)
+    pair = [s.reshape(devices, 8, width) for s in (s0, s2)]
+    x_ref[...] = jnp.concatenate(pair, axis=1).astype(BF16)
     start_all(x_ref, recv, send_a, recv_a)
 
     @pl.when(me < devices - 1)
@@ -315,6 +333,7 @@
     def _():
         send_down.wait_send()
 
+    wait_all(x_mid, recv_mid, send_c, recv_c, False)
     wait_all(x_ref, recv, send_a, recv_a, False)
 
     rows = 16 * BLK
@@ -322,7 +341,9 @@
     def chunk(ch, carry):
         for c in load(ch):
             c.wait()
-        data = recv[...].reshape(devices * BLK, width)
+        data = jnp.concatenate(
+            [ref[...].reshape(devices * 16, width) for ref in (recv_mid, recv)], axis=0
+        )
         coef = jnp.dot(ana[...], data, preferred_element_type=F32)
         gain = gain_ref[pl.ds(pl.multiple_of(ch * CHUNK, CHUNK), CHUNK), :]
         gain = jnp.concatenate([gain] * M_DEV, axis=0)
@@ -347,7 +368,10 @@
     lax.fori_loop(0, chunks, chunk, 0)
     back[...] = acc[...].reshape(devices, BLK, width).astype(BF16)
     start_all(back, ret, send_b, recv_b)
+    wait_all(x_mid, recv_mid, send_c, recv_c, True)
     wait_all(x_ref, recv, send_a, recv_a, True)
+    for c in leave:
+        c.wait()
     wait_all(back, ret, send_b, recv_b, False)
     got = ret[...].astype(F32)
     for i in range(3):
@@ -379,6 +403,7 @@
     shape = jax.ShapeDtypeStruct
     params = functools.partial(pltpu.CompilerParams, vmem_limit_bytes=48 * 2**20)
     block = pltpu.VMEM((devices, BLK, ch), BF16)
+    thin = pltpu.VMEM((devices, 16, ch), BF16)
     cycle = pltpu.VMEM((lon // 8, 16, ch), BF16)
     rows = 2 * M_DEV * CHUNK
     sems = pltpu.SemaphoreType.DMA((devices,))
@@ -386,15 +411,21 @@
     local, modes = pl.pallas_call(
         functools.partial(main_kernel, devices),
         out_shape=(shape((cycles, lon, ch), BF16), shape((3, devices * 8, ch), BF16)),
-        in_specs=[smem, smem, smem, hbm, vmem, vmem, hbm, hbm, vmem, vmem],
-        out_specs=(vmem, vmem),
+        in_specs=[smem, smem, smem] + [hbm] * 7,
+        out_specs=(hbm, vmem),
         scratch_shapes=[
+            pltpu.VMEM((cycles, lon, ch), BF16),
+            pltpu.VMEM(mix.shape, BF16),
+            pltpu.VMEM(fwd.shape, BF16),
+            pltpu.VMEM(gain.shape, F32),
+            pltpu.VMEM(weight.shape, BF16),
+            pltpu.SemaphoreType.DMA((4,)),
+            pltpu.SemaphoreType.DMA((3,)),
             cycle, cycle, cycle, cycle, cycle,
             pltpu.VMEM((3, KB * ROWS, 6 * WIN), BF16),
             pltpu.VMEM((3, lon, KB * ch), BF16),
             pltpu.VMEM((2, lon // ROWS, KB * ROWS, ch), F32),
-            pltpu.VMEM((devices * 8, ch), F32),
-            block, block, block, block,
+            thin, thin, thin, thin, block, block,
             pltpu.VMEM((rows, devices * BLK), BF16),
             pltpu.VMEM((devices * BLK, rows), BF16),
             pltpu.VMEM((2 * ch, 2 * ch), BF16),
@@ -403,9 +434,11 @@
             pltpu.SemaphoreType.DMA((6,)),
             pltpu.SemaphoreType.DMA((2,)),
             pltpu.SemaphoreType.DMA((2,)),
-            sems, sems, sems, sems,
+            sems, sems, sems, sems, sems, sems,
         ],
-        compiler_params=params(collective_id=0, has_side_effects=True),
+        compiler_params=pltpu.CompilerParams(
+            vmem_limit_bytes=60 * 2**20, collective_id=0, has_side_effects=True
+        ),
         name="main",
     )(
         jnp.transpose(filters, (0, 1, 4, 2, 3)), lon // 16 - 1 - turned // 2, 16 - 8 * (turned % 2),

time: 57.5 us -> 56.8 us (0.988)
  local copies, waits for them, and re-layouts: 6.11 us -> 2.55 us
  Pallas kernels: 50.2 us -> 52.7 us
  other arithmetic: 0.7 us -> 1.29 us
    unnamed x14 -> x6, local copies, waits for them, and re-layouts: 6.11 us -> 2.55 us
    pallas_call x1, Pallas kernels: 45.1 us -> 47.6 us  [body(): pl.pallas_call(functools.partial(main_kernel, devices), out_shape=(shape(...]
    sub x1, other arithmetic: 0.7 us -> 1.29 us  [body(): 16 - 8 * (turned % 2)]
where the time goes in v3:
time: 56.8 us; the launch traced here: 56.6 us
  Pallas kernels  52.7 us (93%)
  local copies, waits for them, and re-layouts  2.55 us (4%)
  other arithmetic  1.29 us (2%)
    pallas_call x1, Pallas kernels, body(): pl.pallas_call(functools.partial(main_kernel, devices), out_shape=(shape(...  47.6 us
    pallas_call x1, Pallas kernels, body(): pl.pallas_call(final_kernel, grid=(3, lon // step), out_shape=shape((cycl...  5.13 us
    unnamed x6, local copies, waits for them, and re-layouts  2.55 us
    sub x1, other arithmetic, body(): 16 - 8 * (turned % 2)  1.29 us

profile of v3, /device:TPU:13, one launch (start us, length us, event | category | flops | bytes accessed | tf_op | source)
XLA Modules:
  0.0 56.6 jit_solution(18344202572113920758)
XLA Ops:
  0.0 1.3 %fusion.1 = (s32[3,2,3]{2,1,0:T(2,128)}, s32[3,2,3]{2,1,0:T(2,128)}) fusion(s32[3,3,2]{1,2,0:T(2,128)} %param.12), kind=kLoop, calls=%fused_computation.8 | loop fusion | flops 396 | bytes 216 | tf_op jit(solution)/shard_map/sub | solution.py:444
  1.3 0.0 copy-start.1
  1.3 47.6 %main.1 = (bf16[3,1440,256]{2,1,0:T(8,128)(2,1)}, bf16[3,128,256]{2,1,0:T(8,128)(2,1)}) custom-call(f32[3,3,3,2,8]{4,3,2,1,0:T(2,128)} %bitcast.25, s32[3,2,3]{2,1,0:T(2,128)} %get-tuple-element.10.b_ref, s32[3,2,3]{2,1,0:T(2,128)} %get-tuple-element.9.o_ref, bf16[3,90,16,256]{3,2,1,0:T(8,128)(2,1)} %bitcast.24, bf16[768,256]{1,0:T(8,128)(2,1)} %mix_hbm.1, ...), custom_call_target="tpu_custom_call" | custom-call | tf_op jit(solution)/shard_map/main/pallas_call | solution.py:411
  48.9 0.0 copy-done.1
  48.9 0.0 copy-start
  48.9 1.6 %copy-done = bf16[3,1440,256]{2,1,0:T(8,128)(2,1)S(1)} copy-done((bf16[3,1440,256]{2,1,0:T(8,128)(2,1)S(1)}, bf16[3,1440,256]{2,1,0:T(8,128)(2,1)}, u32[]{:S(2)}) %copy-start) | copy-done | bytes 2211864
  50.5 0.0 copy-start.2
  50.5 0.9 %copy-done.2 = bf16[3,128,256]{2,1,0:T(8,128)(2,1)S(1)} copy-done((bf16[3,128,256]{2,1,0:T(8,128)(2,1)S(1)}, bf16[3,128,256]{2,1,0:T(8,128)(2,1)}, u32[]{:S(2)}) %copy-start.2) | copy-done | bytes 196632
  51.5 5.1 %final.1 = bf16[3,1440,256]{2,1,0:T(8,128)(2,1)} custom-call(bf16[3,1440,256]{2,1,0:T(8,128)(2,1)S(1)} %copy-done, bf16[3,128,256]{2,1,0:T(8,128)(2,1)S(1)} %copy-done.2, bf16[1440,128]{1,0:T(8,128)(2,1)S(1)} %copy-done.1), custom_call_target="tpu_custom_call" | custom-call | tf_op jit(solution)/shard_map/final/pallas_call | solution.py:448
Async XLA Ops:
  1.3 47.6 %copy-start.1 = (bf16[1440,128]{1,0:T(8,128)(2,1)S(1)}, bf16[1440,128]{1,0:T(8,128)(2,1)}, u32[]{:S(2)}) copy-start(bf16[1440,128]{1,0:T(8,128)(2,1)} %constant.41.clone.inv_ref) | copy-start | bytes 1105924
  48.9 1.6 %copy-start = (bf16[3,1440,256]{2,1,0:T(8,128)(2,1)S(1)}, bf16[3,1440,256]{2,1,0:T(8,128)(2,1)}, u32[]{:S(2)}) copy-start(bf16[3,1440,256]{2,1,0:T(8,128)(2,1)} %get-tuple-element.7.local_ref) | copy-start | bytes 6635524
  50.5 0.9 %copy-start.2 = (bf16[3,128,256]{2,1,0:T(8,128)(2,1)S(1)}, bf16[3,128,256]{2,1,0:T(8,128)(2,1)}, u32[]{:S(2)}) copy-start(bf16[3,128,256]{2,1,0:T(8,128)(2,1)} %get-tuple-element.8.modes_ref) | copy-start | bytes 589828

commit v4 on v3

--- a/solution.py
+++ b/solution.py
@@ -310,15 +310,18 @@
 
         ref[tiles : 2 * tiles] = ref[0:tiles]
 
-    def outer(a, carry):
-        first = pl.multiple_of(a * ROWS, 16)
-        for h, ref in enumerate((north, south)):
-            pieces = windows(b_ref, ref, 2 * h, 2 * h, a)
-            basis = jnp.dot(tab[2 * h, :, 4 * WIN :], jnp.concatenate(pieces, axis=0), preferred_element_type=F32)
-            keep(2 * h, first, basis + part[h, a])
+    def outer(group, carry):
+        work = []
+        for a in (3 * group, 3 * group + 1, 3 * group + 2):
+            for h, ref in enumerate((north, south)):
+                data = jnp.concatenate(windows(b_ref, ref, 2 * h, 2 * h, a), axis=0)
+                basis = jnp.dot(tab[2 * h, :, 4 * WIN :], data, preferred_element_type=F32)
+                work.append((h, a, basis + part[h, a]))
+        for h, a, basis in work:
+            keep(2 * h, pl.multiple_of(a * ROWS, 16), basis)
         return carry
 
-    lax.fori_loop(0, lon // ROWS, outer, 0)
+    lax.fori_loop(0, lon // ROWS // 3, outer, 0)
     s0 = mix_cycle(0)
     s2 = mix_cycle(2)
     pair = [s.reshape(devices, 8, width) for s in (s0, s2)]
@@ -401,7 +404,6 @@
     smem = pl.BlockSpec(memory_space=pltpu.SMEM)
     hbm = pl.BlockSpec(memory_space=pl.ANY)
     shape = jax.ShapeDtypeStruct
-    params = functools.partial(pltpu.CompilerParams, vmem_limit_bytes=48 * 2**20)
     block = pltpu.VMEM((devices, BLK, ch), BF16)
     thin = pltpu.VMEM((devices, 16, ch), BF16)
     cycle = pltpu.VMEM((lon // 8, 16, ch), BF16)
@@ -444,7 +446,7 @@
         jnp.transpose(filters, (0, 1, 4, 2, 3)), lon // 16 - 1 - turned // 2, 16 - 8 * (turned % 2),
         state.reshape(cycles, lon // 16, 16, ch), mix, fwd, ana, syn, gain, weight,
     )
-    step = 480
+    step = 720
     return pl.pallas_call(
         final_kernel,
         grid=(3, lon // step),
@@ -455,7 +457,7 @@
             pl.BlockSpec((step, devices * 8), lambda i, n: (n, 0)),
         ],
         out_specs=pl.BlockSpec((1, step, ch), lambda i, n: (i, n, 0)),
-        compiler_params=params(),
+        compiler_params=pltpu.CompilerParams(vmem_limit_bytes=60 * 2**20),
         name="final",
     )(local, modes, inv)
 

time: 56.8 us -> 52.5 us (0.924)
  local copies, waits for them, and re-layouts: 2.55 us -> 0 us
  Pallas kernels: 52.7 us -> 50.7 us
    pallas_call x1, Pallas kernels: 47.6 us -> 44.5 us  [body(): pl.pallas_call(functools.partial(main_kernel, devices), out_shape=(shape(...]
    unnamed x6 -> x0, local copies, waits for them, and re-layouts: 2.55 us -> none
    pallas_call x1, Pallas kernels: 5.13 us -> 6.15 us  [body(): pl.pallas_call(final_kernel, grid=(3, lon // step), out_shape=shape((cycl...]
where the time goes in v4:
time: 52.5 us; the launch traced here: 52 us
  Pallas kernels  50.7 us (97%)
  other arithmetic  1.29 us (2%)
    pallas_call x1, Pallas kernels, body(): pl.pallas_call(functools.partial(main_kernel, devices), out_shape=(shape(...  44.5 us
    pallas_call x1, Pallas kernels, body(): pl.pallas_call(final_kernel, grid=(3, lon // step), out_shape=shape((cycl...  6.15 us
    sub x1, other arithmetic, body(): 16 - 8 * (turned % 2)  1.29 us

profile of v4, /device:TPU:13, one launch (start us, length us, event | category | flops | bytes accessed | tf_op | source)
XLA Modules:
  0.0 52.0 jit_solution(9640586078438417626)
XLA Ops:
  0.0 1.3 %fusion.1 = (s32[3,2,3]{2,1,0:T(2,128)}, s32[3,2,3]{2,1,0:T(2,128)}) fusion(s32[3,3,2]{1,2,0:T(2,128)} %param.12), kind=kLoop, calls=%fused_computation.8 | loop fusion | flops 396 | bytes 216 | tf_op jit(solution)/shard_map/sub | solution.py:446
  1.3 44.5 %main.1 = (bf16[3,1440,256]{2,1,0:T(8,128)(2,1)}, bf16[3,128,256]{2,1,0:T(8,128)(2,1)}) custom-call(f32[3,3,3,2,8]{4,3,2,1,0:T(2,128)} %bitcast.25, s32[3,2,3]{2,1,0:T(2,128)} %get-tuple-element.10.b_ref, s32[3,2,3]{2,1,0:T(2,128)} %get-tuple-element.9.o_ref, bf16[3,90,16,256]{3,2,1,0:T(8,128)(2,1)} %bitcast.24, bf16[768,256]{1,0:T(8,128)(2,1)} %mix_hbm.1, ...), custom_call_target="tpu_custom_call" | custom-call | tf_op jit(solution)/shard_map/main/pallas_call | solution.py:413
  45.8 6.2 %final.1 = bf16[3,1440,256]{2,1,0:T(8,128)(2,1)} custom-call(bf16[3,1440,256]{2,1,0:T(8,128)(2,1)} %get-tuple-element.7.local_ref, bf16[3,128,256]{2,1,0:T(8,128)(2,1)} %get-tuple-element.8.modes_ref, bf16[1440,128]{1,0:T(8,128)(2,1)} %constant.41.clone.inv_ref), custom_call_target="tpu_custom_call" | custom-call | tf_op jit(solution)/shard_map/final/pallas_call | solution.py:450

commit v5 on v4

--- a/solution.py
+++ b/solution.py
@@ -446,7 +446,7 @@
         jnp.transpose(filters, (0, 1, 4, 2, 3)), lon // 16 - 1 - turned // 2, 16 - 8 * (turned % 2),
         state.reshape(cycles, lon // 16, 16, ch), mix, fwd, ana, syn, gain, weight,
     )
-    step = 720
+    step = 480
     return pl.pallas_call(
         final_kernel,
         grid=(3, lon // step),

time: 52.5 us -> 54.4 us (1.036)
  Pallas kernels: 50.7 us -> 52.6 us
    pallas_call x1, Pallas kernels: 6.15 us -> 8.1 us  [body(): pl.pallas_call(final_kernel, grid=(3, lon // step), out_shape=shape((cycl...]
where the time goes in v5:
time: 54.4 us; the launch traced here: 53.9 us
  Pallas kernels  52.6 us (97%)
  other arithmetic  1.29 us (2%)
    pallas_call x1, Pallas kernels, body(): pl.pallas_call(functools.partial(main_kernel, devices), out_shape=(shape(...  44.5 us
    pallas_call x1, Pallas kernels, body(): pl.pallas_call(final_kernel, grid=(3, lon // step), out_shape=shape((cycl...  8.1 us
    sub x1, other arithmetic, body(): 16 - 8 * (turned % 2)  1.29 us

profile of v5, /device:TPU:13, one launch (start us, length us, event | category | flops | bytes accessed | tf_op | source)
XLA Modules:
  0.0 53.9 jit_solution(13433268491033535454)
XLA Ops:
  0.0 1.3 %fusion.1 = (s32[3,2,3]{2,1,0:T(2,128)}, s32[3,2,3]{2,1,0:T(2,128)}) fusion(s32[3,3,2]{1,2,0:T(2,128)} %param.12), kind=kLoop, calls=%fused_computation.8 | loop fusion | flops 396 | bytes 216 | tf_op jit(solution)/shard_map/sub | solution.py:446
  1.3 44.5 %main.1 = (bf16[3,1440,256]{2,1,0:T(8,128)(2,1)}, bf16[3,128,256]{2,1,0:T(8,128)(2,1)}) custom-call(f32[3,3,3,2,8]{4,3,2,1,0:T(2,128)} %bitcast.25, s32[3,2,3]{2,1,0:T(2,128)} %get-tuple-element.10.b_ref, s32[3,2,3]{2,1,0:T(2,128)} %get-tuple-element.9.o_ref, bf16[3,90,16,256]{3,2,1,0:T(8,128)(2,1)} %bitcast.24, bf16[768,256]{1,0:T(8,128)(2,1)} %mix_hbm.1, ...), custom_call_target="tpu_custom_call" | custom-call | tf_op jit(solution)/shard_map/main/pallas_call | solution.py:413
  45.8 8.1 %final.1 = bf16[3,1440,256]{2,1,0:T(8,128)(2,1)} custom-call(bf16[3,1440,256]{2,1,0:T(8,128)(2,1)} %get-tuple-element.7.local_ref, bf16[3,128,256]{2,1,0:T(8,128)(2,1)} %get-tuple-element.8.modes_ref, bf16[1440,128]{1,0:T(8,128)(2,1)} %constant.41.clone.inv_ref), custom_call_target="tpu_custom_call" | custom-call | tf_op jit(solution)/shard_map/final/pallas_call | solution.py:450
